TPU v7x, 128 devices: a whole 4x4x4 slice. The times are simulated.
128 devices in a mesh: au: 8 (over y, z_hi), vert: 16 (over x, z_lo, core).
Axes of the slice: x: 4, y: 4, z: 4 (z_hi: 2, z_lo: 2; z = z_hi * 2 + z_lo), core: 2. Of those that a mesh axis runs over, the one named last changes fastest.
Arguments:
- u_band: float32 [16384, 8192], P(('au', 'vert')), may hold values from -6 to 6
- v_band: float32 [16384, 8192], P(('vert', 'au')), may hold values from -6 to 6
- y_left: float32 [4, 16384, 128], P(None, ('au', 'vert')), may hold values from -0.046875 to 0.046875
- t_left: float32 [4, 128, 128], replicated, may hold values from -3 to 3
- y_right: float32 [4, 16384, 128], P(None, ('vert', 'au')), may hold values from -0.046875 to 0.046875
- t_right: float32 [4, 128, 128], replicated, may hold values from -3 to 3
Outputs:
- u_out: float32 [16384, 8192], P('au', 'vert')
- v_out: float32 [16384, 8192], P('vert', 'au')
All inputs are finite; a program needn't handle non-finite values.
Results may differ from a plain program's by a relative error of at most 0.0001.
Values sent between devices are 32-bit elements; how exact they have to be, the bound alone decides.
A program may use at most 128 MiB of HBM per device.

v0:
```python
import jax
import jax.numpy as jnp
from jax import lax
from jax.sharding import PartitionSpec as P

highest = lax.Precision.HIGHEST


def split_up(value, dim, length):
    before, after = (value.shape[:dim], value.shape[dim + 1 :])
    return jnp.moveaxis(value.reshape(*before, length, -1, *after), dim, 0)


def sent_and_summed(value, axis, dim):
    parts = split_up(value, dim, lax.axis_size(axis))
    arrived = lax.all_to_all(parts, axis, split_axis=0, concat_axis=0, tiled=True)
    return arrived.sum(axis=0)


def from_everyone(value, axis):
    length = lax.axis_size(axis)
    return lax.all_to_all(
        jnp.broadcast_to(value[None], (length, *value.shape)), axis, 0, 0, tiled=True
    )


def in_order(parts, dim):
    parts = jnp.moveaxis(parts, 0, dim)
    lengths = parts.shape
    return parts.reshape(*lengths[:dim], lengths[dim] * lengths[dim + 1], *lengths[dim + 2 :])


def gathered_copies(value, axis, dim):
    parts = from_everyone(value, axis)
    return in_order(parts, dim)


def product(left, right):
    return jnp.dot(left, right, precision=highest, preferred_element_type=jnp.float32)


def project(reflectors, matrix):
    return lax.dot_general(
        reflectors,
        matrix,
        (((0,), (0,)), ((), ())),
        precision=highest,
        preferred_element_type=jnp.float32,
    )


def left_step(matrix, partial_value, reflectors, factor):
    share = sent_and_summed(partial_value, "au", 1)
    scaled = product(factor, share)
    correction = product(reflectors, gathered_copies(scaled, "au", 1))
    return matrix - correction


def right_step(matrix, partial_value, reflectors, factor):
    share = sent_and_summed(partial_value, "vert", 1)
    scaled = product(factor, share)
    correction = product(reflectors, gathered_copies(scaled, "vert", 1))
    return matrix - correction


def shards(u_band, v_band, y_left, t_left, y_right, t_right):
    left_reflectors = lax.all_gather(y_left, "vert", axis=1, tiled=True)
    right_reflectors = gathered_copies(y_right, "au", 1)
    panels = y_left.shape[0]
    left_factors = [jnp.triu(t_left[panel]) for panel in range(panels)]
    right_factors = [jnp.triu(t_right[panel]).T for panel in range(panels)]
    left_plan = [(left_reflectors[panel], left_factors[panel]) for panel in reversed(range(panels))]
    right_plan = [
        (right_reflectors[panel], right_factors[panel]) for panel in reversed(range(panels))
    ]
    left_matrix = lax.all_to_all(u_band, "vert", split_axis=1, concat_axis=0, tiled=True)
    right_matrix = lax.all_to_all(v_band, "au", split_axis=1, concat_axis=0, tiled=True)
    left_first = project(left_plan[0][0], left_matrix)
    right_first = project(right_plan[0][0], right_matrix)
    for position in range(len(left_plan)):
        reflectors, factor = left_plan[position]
        partial_value = left_first if position == 0 else project(reflectors, left_matrix)
        left_matrix = left_step(left_matrix, partial_value, reflectors, factor)
    for position in range(len(right_plan)):
        reflectors, factor = right_plan[position]
        partial_value = right_first if position == 0 else project(reflectors, right_matrix)
        right_matrix = right_step(right_matrix, partial_value, reflectors, factor)
    return (left_matrix, right_matrix)


def solution(mesh):
    return jax.shard_map(
        shards,
        mesh=mesh,
        in_specs=(
            P(("au", "vert"), None),
            P(("vert", "au"), None),
            P(None, ("au", "vert"), None),
            P(),
            P(None, ("vert", "au"), None),
            P(),
        ),
        out_specs=(P("au", "vert"), P("vert", "au")),
        check_vma=False,
    )
```

profile of v0, /device:TPU:1, one launch (start us, length us, event | category | flops | bytes accessed | tf_op | source)
XLA Modules:
  0.0 471.7 jit_solution(7996459752748702852)
XLA Ops:
  7.2 2.5 broadcast_in_dim.34
  9.7 8.3 %all-to-all-start.10 = ((f32[8,4,128,128]{3,2,1,0:T(8,128)}), f32[8,4,128,128]{3,2,1,0:T(8,128)S(1)}, u32[]{:S(2)}, u32[]{:S(2)}) async-start(f32[8,4,128,128]{3,2,1,0:T(8,128)} %broadcast_in_dim.34), calls=%async_computation.10 | async-start | bytes 4194304 | tf_op jit(solution)/shard_map/all_to_all | solution.py:22
  18.0 5.6 %copy.32 = f32[128,8192]{0,1:T(8,128)} copy(f32[128,8192]{1,0:T(8,128)} %param.7) | data formatting | bytes 8388608 | tf_op args[1]
  23.6 24.9 %all-to-all-done.10 = f32[8,4,128,128]{3,2,1,0:T(8,128)S(1)} async-done(((f32[8,4,128,128]{3,2,1,0:T(8,128)}), f32[8,4,128,128]{3,2,1,0:T(8,128)S(1)}, u32[]{:S(2)}, u32[]{:S(2)}) %all-to-all-start.10) | async-done | bytes 2097184 | tf_op jit(solution)/shard_map/all_to_all | solution.py:22
  48.5 4.6 all-to-all-start.9
  53.9 1.2 fusion.47
  55.0 56.6 %all-to-all-done.9 = f32[128,8,1024]{0,2,1:T(8,128)} async-done(((f32[128,8,1024]{0,2,1:T(8,128)}), f32[128,8,1024]{0,2,1:T(8,128)}, u32[]{:S(2)}, u32[]{:S(2)}) %all-to-all-start.9) | async-done | bytes 4194336 | tf_op jit(solution)/shard_map/all_to_all | solution.py:77
  111.7 2.8 copy_bitcast_fusion
  114.5 4.2 convolution_bitcast_fusion
  118.7 6.7 %all-to-all-start.11 = ((f32[16,128,64]{1,2,0:T(8,128)}), f32[16,128,64]{1,2,0:T(8,128)S(1)}, u32[]{:S(2)}, u32[]{:S(2)}) async-start(f32[16,128,64]{1,2,0:T(8,128)} %convolution_bitcast_fusion), calls=%async_computation.11 | async-start | bytes 1048576 | tf_op jit(solution)/shard_map/all_to_all | solution.py:16
  125.5 9.6 %all-to-all-done.11 = f32[16,128,64]{1,2,0:T(8,128)S(1)} async-done(((f32[16,128,64]{1,2,0:T(8,128)}), f32[16,128,64]{1,2,0:T(8,128)S(1)}, u32[]{:S(2)}, u32[]{:S(2)}) %all-to-all-start.11) | async-done | bytes 524320 | tf_op jit(solution)/shard_map/all_to_all | solution.py:16
  135.4 0.8 broadcast_in_dim.35
  136.2 4.7 all-to-all-start.12
  140.9 5.6 %copy.30 = f32[128,8192]{0,1:T(8,128)} copy(f32[128,8192]{1,0:T(8,128)} %param.6) | data formatting | bytes 8388608 | tf_op args[0]
  146.5 4.1 all-to-all-done.12
  150.6 5.6 %all-to-all-start = ((f32[128,16,512]{0,2,1:T(8,128)}), f32[128,16,512]{0,2,1:T(8,128)}, u32[]{:S(2)}, u32[]{:S(2)}) async-start(f32[128,16,512]{0,2,1:T(8,128)} %bitcast.185), calls=%async_computation | async-start | bytes 8388608 | tf_op jit(solution)/shard_map/all_to_all | solution.py:76
  156.3 5.6 %bitcast_subtract_fusion.3 = f32[1024,1024]{0,1:T(8,128)S(1)} fusion(f32[128,1024]{0,1:T(8,128)S(1)} %bitcast.199, f32[1024,128]{1,0:T(8,128)S(1)} %bitcast.195, f32[128,8,1024]{0,2,1:T(8,128)} %all-to-all-done.9), kind=kOutput, calls=%fused_computation.5 | convolution fusion | flops 1611661312 | bytes 9437184 | tf_op jit(solution)/shard_map/dot_general | solution.py:39
  161.9 2.0 copy-done
  163.9 4.3 fusion.48
  168.2 40.8 %all-to-all-done = f32[128,16,512]{0,2,1:T(8,128)} async-done(((f32[128,16,512]{0,2,1:T(8,128)}), f32[128,16,512]{0,2,1:T(8,128)}, u32[]{:S(2)}, u32[]{:S(2)}) %all-to-all-start) | async-done | bytes 4194336 | tf_op jit(solution)/shard_map/all_to_all | solution.py:76
  209.0 23.0 %all-to-all-start.13 = ((f32[16,128,64]{1,2,0:T(8,128)}), f32[16,128,64]{1,2,0:T(8,128)S(1)}, u32[]{:S(2)}, u32[]{:S(2)}) async-start(f32[16,128,64]{1,2,0:T(8,128)} %bitcast.51), calls=%async_computation.13 | async-start | bytes 1048576 | tf_op jit(solution)/shard_map/all_to_all | solution.py:16
  232.0 4.8 %copy_bitcast_fusion.1 = f32[2048,512]{0,1:T(8,128)} fusion(f32[128,16,512]{0,2,1:T(8,128)} %all-to-all-done), kind=kLoop, calls=%fused_computation.1 | loop fusion | bytes 8388608 | tf_op jit(solution)/shard_map/all_to_all | solution.py:76
  236.8 6.7 %convolution_bitcast_fusion.1 = f32[8,128,64]{1,2,0:T(8,128)} fusion(f32[8,64,2048]{2,1,0:T(8,128)} %bitcast.186, f32[4,2048,128]{2,1,0:T(8,128)} %all-gather.2.cloned.1.call-done), kind=kOutput, calls=%fused_computation.11 | convolution fusion | flops 1610612736 | bytes 5505024 | tf_op jit(solution)/shard_map/dot_general | solution.py:43
  243.4 4.8 %all-to-all-start.1 = ((f32[8,128,64]{1,2,0:T(8,128)}), f32[8,128,64]{1,2,0:T(8,128)S(1)}, u32[]{:S(2)}, u32[]{:S(2)}) async-start(f32[8,128,64]{1,2,0:T(8,128)} %convolution_bitcast_fusion.1), calls=%async_computation.1 | async-start | bytes 524288 | tf_op jit(solution)/shard_map/all_to_all | solution.py:16
  248.5 7.8 %all-to-all-done.1 = f32[8,128,64]{1,2,0:T(8,128)S(1)} async-done(((f32[8,128,64]{1,2,0:T(8,128)}), f32[8,128,64]{1,2,0:T(8,128)S(1)}, u32[]{:S(2)}, u32[]{:S(2)}) %all-to-all-start.1) | async-done | bytes 262176 | tf_op jit(solution)/shard_map/all_to_all | solution.py:16
  257.1 6.1 %all-to-all-start.14 = ((f32[16,128,64]{1,2,0:T(8,128)}), f32[16,128,64]{1,2,0:T(8,128)S(1)}, u32[]{:S(2)}, u32[]{:S(2)}) async-start(f32[16,128,64]{1,2,0:T(8,128)} %broadcast_in_dim.36), calls=%async_computation.14 | async-start | bytes 1048576 | tf_op jit(solution)/shard_map/all_to_all | solution.py:22
  263.6 9.3 %all-to-all-done.14 = f32[16,128,64]{1,2,0:T(8,128)S(1)} async-done(((f32[16,128,64]{1,2,0:T(8,128)}), f32[16,128,64]{1,2,0:T(8,128)S(1)}, u32[]{:S(2)}, u32[]{:S(2)}) %all-to-all-start.14) | async-done | bytes 524320 | tf_op jit(solution)/shard_map/all_to_all | solution.py:22
  273.6 3.4 all-to-all-start.2
  277.0 6.5 %bitcast_subtract_fusion.2 = f32[1024,1024]{0,1:T(8,128)} fusion(f32[1024,1024]{0,1:T(8,128)} %copy-done, f32[128,1024]{0,1:T(8,128)S(1)} %bitcast.197, f32[1024,128]{1,0:T(8,128)S(1)} %bitcast.193), kind=kOutput, calls=%fused_computation.4 | convolution fusion | flops 1611661312 | bytes 9437184 | tf_op jit(solution)/shard_map/dot_general | solution.py:39
  284.3 5.6 %bitcast_subtract_fusion.7 = f32[2048,512]{0,1:T(8,128)S(1)} fusion(f32[128,512]{0,1:T(8,128)S(1)} %bitcast.203, f32[4,2048,128]{2,1,0:T(8,128)} %all-gather.2.cloned.1.call-done, f32[128,16,512]{0,2,1:T(8,128)} %all-to-all-done), kind=kOutput, calls=%fused_computation.9 | convolution fusion | flops 1611661312 | bytes 9699328 | tf_op jit(solution)/shard_map/dot_general | solution.py:39
  289.9 2.0 copy-done.2
  291.9 5.4 %fusion.2 = f32[512,128]{1,0:T(8,128)} fusion(f32[2048,512]{0,1:T(8,128)S(1)} %bitcast_subtract_fusion.7, f32[4,2048,128]{2,1,0:T(8,128)} %all-gather.2.cloned.1.call-done), kind=kOutput, calls=%fused_computation.17 | convolution fusion | flops 1610612736 | bytes 5505024 | tf_op jit(solution)/shard_map/dot_general | solution.py:43
  297.2 5.9 %all-to-all-start.3 = ((f32[8,128,64]{1,2,0:T(8,128)}), f32[8,128,64]{1,2,0:T(8,128)S(1)}, u32[]{:S(2)}, u32[]{:S(2)}) async-start(f32[8,128,64]{1,2,0:T(8,128)} %bitcast.15), calls=%async_computation.3 | async-start | bytes 524288 | tf_op jit(solution)/shard_map/all_to_all | solution.py:16
  303.1 6.4 %fusion.49 = f32[1024,128]{1,0:T(8,128)} fusion(f32[1024,1024]{0,1:T(8,128)} %bitcast_subtract_fusion.2, f32[1024,128]{1,0:T(8,128)S(1)} %bitcast.190), kind=kOutput, calls=%fused_computation.74 | convolution fusion | flops 1610612736 | bytes 5242880 | tf_op jit(solution)/shard_map/dot_general | solution.py:43
  309.5 0.9 all-to-all-done.3
  310.5 6.6 %all-to-all-start.15 = ((f32[16,128,64]{1,2,0:T(8,128)}), f32[16,128,64]{1,2,0:T(8,128)S(1)}, u32[]{:S(2)}, u32[]{:S(2)}) async-start(f32[16,128,64]{1,2,0:T(8,128)} %bitcast.59), calls=%async_computation.15 | async-start | bytes 1048576 | tf_op jit(solution)/shard_map/all_to_all | solution.py:16
  317.4 9.3 %all-to-all-done.15 = f32[16,128,64]{1,2,0:T(8,128)S(1)} async-done(((f32[16,128,64]{1,2,0:T(8,128)}), f32[16,128,64]{1,2,0:T(8,128)S(1)}, u32[]{:S(2)}, u32[]{:S(2)}) %all-to-all-start.15) | async-done | bytes 524320 | tf_op jit(solution)/shard_map/all_to_all | solution.py:16
  327.5 4.9 %all-to-all-start.4 = ((f32[8,128,64]{1,2,0:T(8,128)}), f32[8,128,64]{1,2,0:T(8,128)S(1)}, u32[]{:S(2)}, u32[]{:S(2)}) async-start(f32[8,128,64]{1,2,0:T(8,128)} %broadcast_in_dim.31), calls=%async_computation.4 | async-start | bytes 524288 | tf_op jit(solution)/shard_map/all_to_all | solution.py:22
  332.7 7.0 %all-to-all-done.4 = f32[8,128,64]{1,2,0:T(8,128)S(1)} async-done(((f32[8,128,64]{1,2,0:T(8,128)}), f32[8,128,64]{1,2,0:T(8,128)S(1)}, u32[]{:S(2)}, u32[]{:S(2)}) %all-to-all-start.4) | async-done | bytes 262176 | tf_op jit(solution)/shard_map/all_to_all | solution.py:22
  339.7 0.9 broadcast_in_dim.37
  340.6 6.5 %all-to-all-start.16 = ((f32[16,128,64]{1,2,0:T(8,128)}), f32[16,128,64]{1,2,0:T(8,128)S(1)}, u32[]{:S(2)}, u32[]{:S(2)}) async-start(f32[16,128,64]{1,2,0:T(8,128)} %broadcast_in_dim.37), calls=%async_computation.16 | async-start | bytes 1048576 | tf_op jit(solution)/shard_map/all_to_all | solution.py:22
  347.1 5.7 %bitcast_subtract_fusion.6 = f32[2048,512]{0,1:T(8,128)S(1)} fusion(f32[2048,512]{0,1:T(8,128)} %copy-done.2, f32[128,512]{0,1:T(8,128)S(1)} %bitcast.200, f32[4,2048,128]{2,1,0:T(8,128)} %all-gather.2.cloned.1.call-done), kind=kOutput, calls=%fused_computation.8 | convolution fusion | flops 1611661312 | bytes 9699328 | tf_op jit(solution)/shard_map/dot_general | solution.py:39
  352.9 2.0 copy-done.3
  354.9 5.4 %fusion.3 = f32[512,128]{1,0:T(8,128)} fusion(f32[2048,512]{0,1:T(8,128)S(1)} %bitcast_subtract_fusion.6, f32[4,2048,128]{2,1,0:T(8,128)} %all-gather.2.cloned.1.call-done), kind=kOutput, calls=%fused_computation.18 | convolution fusion | flops 1610612736 | bytes 5505024 | tf_op jit(solution)/shard_map/dot_general | solution.py:43
  360.2 3.4 all-to-all-start.5
  363.7 6.6 %bitcast_subtract_fusion.1 = f32[1024,1024]{0,1:T(8,128)} fusion(f32[1024,1024]{0,1:T(8,128)} %bitcast_subtract_fusion.2, f32[128,1024]{0,1:T(8,128)S(1)} %bitcast.198, f32[1024,128]{1,0:T(8,128)S(1)} %bitcast.191), kind=kOutput, calls=%fused_computation.3 | convolution fusion | flops 1611661312 | bytes 9437184 | tf_op jit(solution)/shard_map/dot_general | solution.py:39
  370.3 1.6 all-to-all-done.5
  373.0 4.9 %all-to-all-start.6 = ((f32[8,128,64]{1,2,0:T(8,128)}), f32[8,128,64]{1,2,0:T(8,128)S(1)}, u32[]{:S(2)}, u32[]{:S(2)}) async-start(f32[8,128,64]{1,2,0:T(8,128)} %broadcast_in_dim.32), calls=%async_computation.6 | async-start | bytes 524288 | tf_op jit(solution)/shard_map/all_to_all | solution.py:22
  377.9 6.5 %fusion.50 = f32[1024,128]{1,0:T(8,128)} fusion(f32[1024,1024]{0,1:T(8,128)} %bitcast_subtract_fusion.1, f32[1024,128]{1,0:T(8,128)S(1)} %bitcast.188), kind=kOutput, calls=%fused_computation.75 | convolution fusion | flops 1610612736 | bytes 5242880 | tf_op jit(solution)/shard_map/dot_general | solution.py:43
  384.4 1.0 all-to-all-done.6
  385.4 7.9 %all-to-all-start.17 = ((f32[16,128,64]{1,2,0:T(8,128)}), f32[16,128,64]{1,2,0:T(8,128)S(1)}, u32[]{:S(2)}, u32[]{:S(2)}) async-start(f32[16,128,64]{1,2,0:T(8,128)} %bitcast.67), calls=%async_computation.17 | async-start | bytes 1048576 | tf_op jit(solution)/shard_map/all_to_all | solution.py:16
  393.3 5.8 %bitcast_subtract_fusion.5 = f32[2048,512]{0,1:T(8,128)S(1)} fusion(f32[2048,512]{0,1:T(8,128)} %copy-done.3, f32[128,512]{0,1:T(8,128)S(1)} %bitcast.201, f32[4,2048,128]{2,1,0:T(8,128)} %all-gather.2.cloned.1.call-done), kind=kOutput, calls=%fused_computation.7 | convolution fusion | flops 1611661312 | bytes 9699328 | tf_op jit(solution)/shard_map/dot_general | solution.py:39
  399.1 2.0 copy-done.1
  401.1 5.4 %fusion.4 = f32[512,128]{1,0:T(8,128)} fusion(f32[2048,512]{0,1:T(8,128)S(1)} %bitcast_subtract_fusion.5, f32[4,2048,128]{2,1,0:T(8,128)} %all-gather.2.cloned.1.call-done), kind=kOutput, calls=%fused_computation.19 | convolution fusion | flops 1610612736 | bytes 5505024 | tf_op jit(solution)/shard_map/dot_general | solution.py:43
  406.4 5.2 %all-to-all-start.7 = ((f32[8,128,64]{1,2,0:T(8,128)}), f32[8,128,64]{1,2,0:T(8,128)S(1)}, u32[]{:S(2)}, u32[]{:S(2)}) async-start(f32[8,128,64]{1,2,0:T(8,128)} %bitcast.31), calls=%async_computation.7 | async-start | bytes 524288 | tf_op jit(solution)/shard_map/all_to_all | solution.py:16
  412.0 7.9 %all-to-all-done.7 = f32[8,128,64]{1,2,0:T(8,128)S(1)} async-done(((f32[8,128,64]{1,2,0:T(8,128)}), f32[8,128,64]{1,2,0:T(8,128)S(1)}, u32[]{:S(2)}, u32[]{:S(2)}) %all-to-all-start.7) | async-done | bytes 262176 | tf_op jit(solution)/shard_map/all_to_all | solution.py:16
  419.9 0.8 broadcast_in_dim.74
  420.7 6.0 %all-to-all-start.18 = ((f32[16,128,64]{1,2,0:T(8,128)}), f32[16,128,64]{1,2,0:T(8,128)S(1)}, u32[]{:S(2)}, u32[]{:S(2)}) async-start(f32[16,128,64]{1,2,0:T(8,128)} %broadcast_in_dim.74), calls=%async_computation.18 | async-start | bytes 1048576 | tf_op jit(solution)/shard_map/all_to_all | solution.py:22
  427.0 9.3 %all-to-all-done.18 = f32[16,128,64]{1,2,0:T(8,128)S(1)} async-done(((f32[16,128,64]{1,2,0:T(8,128)}), f32[16,128,64]{1,2,0:T(8,128)S(1)}, u32[]{:S(2)}, u32[]{:S(2)}) %all-to-all-start.18) | async-done | bytes 524320 | tf_op jit(solution)/shard_map/all_to_all | solution.py:22
  437.1 3.4 all-to-all-start.8
  440.5 6.6 %bitcast_subtract_fusion = f32[1024,1024]{0,1:T(8,128)} fusion(f32[1024,1024]{0,1:T(8,128)} %bitcast_subtract_fusion.1, f32[128,1024]{0,1:T(8,128)S(1)} %bitcast.196, f32[1024,128]{1,0:T(8,128)S(1)} %bitcast.189), kind=kOutput, calls=%fused_computation.2 | convolution fusion | flops 1611661312 | bytes 9437184 | tf_op jit(solution)/shard_map/dot_general | solution.py:39
  447.1 5.3 %copy.35 = f32[1024,1024]{1,0:T(8,128)} copy(f32[1024,1024]{0,1:T(8,128)} %bitcast_subtract_fusion) | data formatting | bytes 8388608
  452.4 6.9 %bitcast_subtract_fusion.4 = f32[2048,512]{0,1:T(8,128)} fusion(f32[2048,512]{0,1:T(8,128)} %copy-done.1, f32[128,512]{0,1:T(8,128)S(1)} %bitcast.202, f32[4,2048,128]{2,1,0:T(8,128)} %all-gather.2.cloned.1.call-done), kind=kOutput, calls=%fused_computation.6 | convolution fusion | flops 1611661312 | bytes 9699328 | tf_op jit(solution)/shard_map/dot_general | solution.py:39
  459.3 5.3 %copy.34 = f32[2048,512]{1,0:T(8,128)} copy(f32[2048,512]{0,1:T(8,128)} %bitcast_subtract_fusion.4) | data formatting | bytes 8388608
  (42 shorter events, 7.7 us)
Async XLA Ops:
  9.7 38.8 %all-to-all-start.10 = ((f32[8,4,128,128]{3,2,1,0:T(8,128)}), f32[8,4,128,128]{3,2,1,0:T(8,128)S(1)}, u32[]{:S(2)}, u32[]{:S(2)}) async-start(f32[8,4,128,128]{3,2,1,0:T(8,128)} %broadcast_in_dim.34), calls=%async_computation.10 | async-start | bytes 4194304 | tf_op jit(solution)/shard_map/all_to_all | solution.py:22
  48.5 63.1 %all-to-all-start.9 = ((f32[128,8,1024]{0,2,1:T(8,128)}), f32[128,8,1024]{0,2,1:T(8,128)}, u32[]{:S(2)}, u32[]{:S(2)}) async-start(f32[128,8,1024]{0,2,1:T(8,128)} %bitcast.184), calls=%async_computation.9 | async-start | bytes 8388608 | tf_op jit(solution)/shard_map/all_to_all | solution.py:77
  53.1 183.6 %all-gather.2.cloned.1.call-start = ((), (), s32[]{:S(2)}) async-start(), calls=%async_computation.19 | async-start | bytes 4456448 | tf_op jit(solution)/shard_map/all_gather | solution.py:67
  55.0 59.5 %copy-start.5 = (f32[1,8,128,128]{3,2,0,1:T(8,128)S(1)}, f32[1,8,128,128]{3,2,0,1:T(8,128)}, u32[]{:S(2)}) copy-start(f32[1,8,128,128]{3,2,0,1:T(8,128)} %get-tuple-element.13) | copy-start | bytes 1572868
  114.5 20.6 %copy-start.6 = (f32[4,128,128]{2,1,0:T(8,128)S(1)}, f32[4,128,128]{2,1,0:T(8,128)}, u32[]{:S(2)}) copy-start(f32[4,128,128]{2,1,0:T(8,128)} %param.11) | copy-start | bytes 786436
  118.7 16.4 %all-to-all-start.11 = ((f32[16,128,64]{1,2,0:T(8,128)}), f32[16,128,64]{1,2,0:T(8,128)S(1)}, u32[]{:S(2)}, u32[]{:S(2)}) async-start(f32[16,128,64]{1,2,0:T(8,128)} %convolution_bitcast_fusion), calls=%async_computation.11 | async-start | bytes 1048576 | tf_op jit(solution)/shard_map/all_to_all | solution.py:16
  136.2 14.4 %all-to-all-start.12 = ((f32[16,128,64]{1,2,0:T(8,128)}), f32[16,128,64]{1,2,0:T(8,128)S(1)}, u32[]{:S(2)}, u32[]{:S(2)}) async-start(f32[16,128,64]{1,2,0:T(8,128)} %broadcast_in_dim.35), calls=%async_computation.12 | async-start | bytes 1048576 | tf_op jit(solution)/shard_map/all_to_all | solution.py:22
  150.6 58.4 %all-to-all-start = ((f32[128,16,512]{0,2,1:T(8,128)}), f32[128,16,512]{0,2,1:T(8,128)}, u32[]{:S(2)}, u32[]{:S(2)}) async-start(f32[128,16,512]{0,2,1:T(8,128)} %bitcast.185), calls=%async_computation | async-start | bytes 8388608 | tf_op jit(solution)/shard_map/all_to_all | solution.py:76
  156.3 7.6 %copy-start.4 = (f32[1,8,128,128]{3,2,0,1:T(8,128)S(1)}, f32[1,8,128,128]{3,2,0,1:T(8,128)}, u32[]{:S(2)}) copy-start(f32[1,8,128,128]{3,2,0,1:T(8,128)} %get-tuple-element.12) | copy-start | bytes 1572868
  161.9 2.0 copy-start
  209.0 34.4 %all-to-all-start.13 = ((f32[16,128,64]{1,2,0:T(8,128)}), f32[16,128,64]{1,2,0:T(8,128)S(1)}, u32[]{:S(2)}, u32[]{:S(2)}) async-start(f32[16,128,64]{1,2,0:T(8,128)} %bitcast.51), calls=%async_computation.13 | async-start | bytes 1048576 | tf_op jit(solution)/shard_map/all_to_all | solution.py:16
  236.8 26.5 %copy-start.7 = (f32[4,128,128]{2,1,0:T(8,128)S(1)}, f32[4,128,128]{2,1,0:T(8,128)}, u32[]{:S(2)}) copy-start(f32[4,128,128]{2,1,0:T(8,128)} %param.9) | copy-start | bytes 786436
  243.4 12.9 %all-to-all-start.1 = ((f32[8,128,64]{1,2,0:T(8,128)}), f32[8,128,64]{1,2,0:T(8,128)S(1)}, u32[]{:S(2)}, u32[]{:S(2)}) async-start(f32[8,128,64]{1,2,0:T(8,128)} %convolution_bitcast_fusion.1), calls=%async_computation.1 | async-start | bytes 524288 | tf_op jit(solution)/shard_map/all_to_all | solution.py:16
  257.1 15.7 %all-to-all-start.14 = ((f32[16,128,64]{1,2,0:T(8,128)}), f32[16,128,64]{1,2,0:T(8,128)S(1)}, u32[]{:S(2)}, u32[]{:S(2)}) async-start(f32[16,128,64]{1,2,0:T(8,128)} %broadcast_in_dim.36), calls=%async_computation.14 | async-start | bytes 1048576 | tf_op jit(solution)/shard_map/all_to_all | solution.py:22
  273.6 10.7 %all-to-all-start.2 = ((f32[8,128,64]{1,2,0:T(8,128)}), f32[8,128,64]{1,2,0:T(8,128)S(1)}, u32[]{:S(2)}, u32[]{:S(2)}) async-start(f32[8,128,64]{1,2,0:T(8,128)} %broadcast_in_dim.30), calls=%async_computation.2 | async-start | bytes 524288 | tf_op jit(solution)/shard_map/all_to_all | solution.py:22
  289.9 2.0 copy-start.2
  297.2 13.2 %all-to-all-start.3 = ((f32[8,128,64]{1,2,0:T(8,128)}), f32[8,128,64]{1,2,0:T(8,128)S(1)}, u32[]{:S(2)}, u32[]{:S(2)}) async-start(f32[8,128,64]{1,2,0:T(8,128)} %bitcast.15), calls=%async_computation.3 | async-start | bytes 524288 | tf_op jit(solution)/shard_map/all_to_all | solution.py:16
  310.5 16.3 %all-to-all-start.15 = ((f32[16,128,64]{1,2,0:T(8,128)}), f32[16,128,64]{1,2,0:T(8,128)S(1)}, u32[]{:S(2)}, u32[]{:S(2)}) async-start(f32[16,128,64]{1,2,0:T(8,128)} %bitcast.59), calls=%async_computation.15 | async-start | bytes 1048576 | tf_op jit(solution)/shard_map/all_to_all | solution.py:16
  327.5 12.2 %all-to-all-start.4 = ((f32[8,128,64]{1,2,0:T(8,128)}), f32[8,128,64]{1,2,0:T(8,128)S(1)}, u32[]{:S(2)}, u32[]{:S(2)}) async-start(f32[8,128,64]{1,2,0:T(8,128)} %broadcast_in_dim.31), calls=%async_computation.4 | async-start | bytes 524288 | tf_op jit(solution)/shard_map/all_to_all | solution.py:22
  340.6 19.7 %all-to-all-start.16 = ((f32[16,128,64]{1,2,0:T(8,128)}), f32[16,128,64]{1,2,0:T(8,128)S(1)}, u32[]{:S(2)}, u32[]{:S(2)}) async-start(f32[16,128,64]{1,2,0:T(8,128)} %broadcast_in_dim.37), calls=%async_computation.16 | async-start | bytes 1048576 | tf_op jit(solution)/shard_map/all_to_all | solution.py:22
  352.9 2.0 copy-start.3
  360.2 11.7 %all-to-all-start.5 = ((f32[8,128,64]{1,2,0:T(8,128)}), f32[8,128,64]{1,2,0:T(8,128)S(1)}, u32[]{:S(2)}, u32[]{:S(2)}) async-start(f32[8,128,64]{1,2,0:T(8,128)} %bitcast.23), calls=%async_computation.5 | async-start | bytes 524288 | tf_op jit(solution)/shard_map/all_to_all | solution.py:16
  373.0 12.4 %all-to-all-start.6 = ((f32[8,128,64]{1,2,0:T(8,128)}), f32[8,128,64]{1,2,0:T(8,128)S(1)}, u32[]{:S(2)}, u32[]{:S(2)}) async-start(f32[8,128,64]{1,2,0:T(8,128)} %broadcast_in_dim.32), calls=%async_computation.6 | async-start | bytes 524288 | tf_op jit(solution)/shard_map/all_to_all | solution.py:22
  385.4 21.1 %all-to-all-start.17 = ((f32[16,128,64]{1,2,0:T(8,128)}), f32[16,128,64]{1,2,0:T(8,128)S(1)}, u32[]{:S(2)}, u32[]{:S(2)}) async-start(f32[16,128,64]{1,2,0:T(8,128)} %bitcast.67), calls=%async_computation.17 | async-start | bytes 1048576 | tf_op jit(solution)/shard_map/all_to_all | solution.py:16
  399.0 2.0 copy-start.1
  406.4 13.5 %all-to-all-start.7 = ((f32[8,128,64]{1,2,0:T(8,128)}), f32[8,128,64]{1,2,0:T(8,128)S(1)}, u32[]{:S(2)}, u32[]{:S(2)}) async-start(f32[8,128,64]{1,2,0:T(8,128)} %bitcast.31), calls=%async_computation.7 | async-start | bytes 524288 | tf_op jit(solution)/shard_map/all_to_all | solution.py:16
  420.7 15.6 %all-to-all-start.18 = ((f32[16,128,64]{1,2,0:T(8,128)}), f32[16,128,64]{1,2,0:T(8,128)S(1)}, u32[]{:S(2)}, u32[]{:S(2)}) async-start(f32[16,128,64]{1,2,0:T(8,128)} %broadcast_in_dim.74), calls=%async_computation.18 | async-start | bytes 1048576 | tf_op jit(solution)/shard_map/all_to_all | solution.py:22
  437.1 15.4 %all-to-all-start.8 = ((f32[8,128,64]{1,2,0:T(8,128)}), f32[8,128,64]{1,2,0:T(8,128)S(1)}, u32[]{:S(2)}, u32[]{:S(2)}) async-start(f32[8,128,64]{1,2,0:T(8,128)} %broadcast_in_dim.33), calls=%async_computation.8 | async-start | bytes 524288 | tf_op jit(solution)/shard_map/all_to_all | solution.py:22
Sparse Core Ops, SparseCore 0:
  55.6 69.0 all-gather.1
where the time goes:
time: 477 us; the launch traced here: 472 us
  waiting for transfers between devices  192 us (40%)
  starting transfers between devices  122 us (26%)
  matrix products  95.7 us (20%)
  local copies, waits for them, and re-layouts  47.4 us (10%)
  between operations  14.5 us (3%)
    all_to_all x8, starting transfers between devices, sent_and_summed(): lax.all_to_all(parts, axis, split_axis=0, concat_axis=0, tiled=True)  63.6 us
    all_to_all x1, waiting for transfers between devices, shards(): lax.all_to_all(v_band, 'au', split_axis=1, concat_axis=0, tiled=True)  56.6 us
    all_to_all x9, waiting for transfers between devices, from_everyone(): lax.all_to_all(jnp.broadcast_to(value[None], (length, *value.shape)), axi...  56.3 us
    dot_general x16, matrix products, product(): jnp.dot(left, right, precision=highest, preferred_element_type=jnp.float32)  51.6 us
    all_to_all x9, starting transfers between devices, from_everyone(): lax.all_to_all(jnp.broadcast_to(value[None], (length, *value.shape)), axi...  48.3 us
    dot_general x8, matrix products, project(): lax.dot_general(reflectors, matrix, (((0,), (0,)), ((), ())), precision=h...  44.1 us
    all_to_all x1, waiting for transfers between devices, shards(): lax.all_to_all(u_band, 'vert', split_axis=1, concat_axis=0, tiled=True)  40.8 us
    all_to_all x8, waiting for transfers between devices, sent_and_summed(): lax.all_to_all(parts, axis, split_axis=0, concat_axis=0, tiled=True)  37.3 us
  transfers between devices with their start and end apart: 20, of which 15 were waited for; matrix products, arithmetic and copies ran while one was open for 22% of the time, Pallas kernels for 0%

commit v1 on v0

v1 whole, which is shorter than its diff:
```python
import functools

import jax
import jax.numpy as jnp
from jax import lax
from jax.experimental import pallas as pl
from jax.experimental.pallas import tpu as pltpu
from jax.sharding import PartitionSpec as P

MESH = pl.DeviceIdType.MESH
f32 = jnp.float32
bf16 = jnp.bfloat16
PAIRS = [(0, 1), (0, 2), (0, 3), (1, 2), (1, 3), (2, 3)]
VERT_OFFSETS = [(dx, dz, dc) for dx in (2, 1, 3, 0) for dz in (1, 0) for dc in (0, 1)][:-2] + [(0, 0, 1)]


def split(value):
    high = value.astype(bf16)
    return high, (value - high.astype(f32)).astype(bf16)


def dot(a, b):
    return lax.dot_general(a, b, (((1,), (0,)), ((), ())), preferred_element_type=f32)


def dot_t(a, b):
    return lax.dot_general(a, b, (((1,), (1,)), ((), ())), preferred_element_type=f32)


def three(a_high, a_low, b_high, b_low, product=dot):
    return product(a_high, b_high) + product(a_high, b_low) + product(a_low, b_high)


def exact(a, b):
    return jnp.dot(a, b, precision=lax.Precision.HIGHEST, preferred_element_type=f32)


def aligned(index, size):
    return pl.ds(pl.multiple_of(index * size, size), size)


def gram_kernel(yl, yr, out):
    for side, y in enumerate((yl, yr)):
        for place, (p, q) in enumerate(PAIRS):
            out[side * 6 + place] = exact(y[p].T, y[q])


def flat(offset):
    dx, dz, dc = offset
    return dx * 4 + dz * 2 + dc


def back(offset):
    dx, dz, dc = offset
    return ((4 - dx) % 4, dz, dc)


def move_kernel(
    yl, yr, u, v,
    u_out, v_out, yl_out, yr_out, sl_out, sr_out,
    ubuf, vbuf, ylbuf, yrbuf, ylt_h, ylt_l, yrt_h, yrt_l, acc,
    spr, core_in, x_in, shr, zl_in, sfr,
    spl, y_in, shl, zh_in, sfl,
    lsem, osem, yls, ylr, yrs, yrr, us, ur, vs, vr,
    rs, rr, ls, lr,
):
    a = lax.axis_index("au")
    t = lax.axis_index("vert")
    y, zh = a // 2, a % 2
    x, zl, c = t // 4, (t // 2) % 2, t % 2

    def vpos(dx, dz, dc):
        return lax.rem(x + dx, 4) * 4 + lax.rem(zl + dz, 2) * 2 + lax.rem(c + dc, 2)

    def apos(dy, dz):
        return lax.rem(y + dy, 4) * 2 + lax.rem(zh + dz, 2)

    sent = []

    def send(src, dst, ssem, rsem, device):
        copy = pltpu.make_async_remote_copy(
            src_ref=src, dst_ref=dst, send_sem=ssem, recv_sem=rsem,
            device_id=device, device_id_type=MESH,
        )
        copy.start()
        sent.append(copy)

    def arrive(dst, ssem, rsem):
        pltpu.make_async_remote_copy(
            src_ref=dst, dst_ref=dst, send_sem=ssem, recv_sem=rsem,
            device_id=(a, t), device_id_type=MESH,
        ).wait_recv()

    locals_y = []
    for p in range(4):
        locals_y.append(pltpu.make_async_copy(
            yl.at[p], ylbuf.at[aligned(t, 128), pl.ds(p * 128, 128)], lsem.at[p]))
        locals_y.append(pltpu.make_async_copy(
            yr.at[p], yrbuf.at[aligned(a, 128), pl.ds(p * 128, 128)], lsem.at[4 + p]))
    local_u = pltpu.make_async_copy(u.at[:, aligned(t, 512)], ubuf.at[aligned(t, 128), :], lsem.at[8])
    local_v = pltpu.make_async_copy(v.at[:, aligned(a, 1024)], vbuf.at[aligned(a, 128), :], lsem.at[9])
    for copy in locals_y + [local_u, local_v]:
        copy.start()

    barrier = pltpu.get_barrier_semaphore()
    for offset in VERT_OFFSETS:
        pl.semaphore_signal(barrier, inc=1, device_id=(a, vpos(*offset)), device_id_type=MESH)
    for o in range(1, 8):
        pl.semaphore_signal(barrier, inc=1, device_id=(apos(o // 2, o % 2), t), device_id_type=MESH)
    pl.semaphore_wait(barrier, 22)

    for copy in locals_y:
        copy.wait()

    def yl_slot(dx, dz, dc):
        return ylbuf.at[aligned(vpos(dx, dz, dc), 128), :]

    def yr_slot(dy, dz):
        return yrbuf.at[aligned(apos(dy, dz), 128), :]

    own = yl_slot(0, 0, 0)
    send(own, own, yls.at[0], ylr.at[2], (a, vpos(0, 1, 0)))
    for dx in (1, 2, 3):
        send(own, own, yls.at[dx], ylr.at[((4 - dx) % 4) * 4], (a, vpos(dx, 0, 0)))
    send(own, own, yls.at[7], ylr.at[1], (a, vpos(0, 0, 1)))
    mine = yr_slot(0, 0)
    send(mine, mine, yrs.at[0], yrr.at[1], (apos(0, 1), t))
    for dy in (1, 2, 3):
        send(mine, mine, yrs.at[dy], yrr.at[((4 - dy) % 4) * 2], (apos(dy, 0), t))

    for o in (5, 4, 3, 2, 7, 6, 1):
        dy, dz = o // 2, o % 2
        target = apos(dy, dz)
        send(v.at[:, aligned(target, 1024)], vbuf.at[aligned(a, 128), :],
             vs.at[o], vr.at[((4 - dy) % 4) * 2 + dz], (target, t))
    for part in range(2):
        for offset in VERT_OFFSETS:
            target = vpos(*offset)
            send(u.at[:, pl.ds(pl.multiple_of(target * 512 + part * 256, 256), 256)],
                 ubuf.at[aligned(t, 128), pl.ds(part * 256, 256)],
                 us.at[part, flat(offset)], ur.at[part, flat(back(offset))], (a, target))

    slot = yl_slot(0, 1, 0)
    arrive(slot, yls.at[0], ylr.at[2])
    for dx in (1, 2, 3):
        send(slot, slot, yls.at[3 + dx], ylr.at[((4 - dx) % 4) * 4 + 2], (a, vpos(dx, 0, 0)))
    send(slot, slot, yls.at[8], ylr.at[3], (a, vpos(0, 0, 1)))
    slot = yr_slot(0, 1)
    arrive(slot, yrs.at[0], yrr.at[1])
    for dy in (1, 2, 3):
        send(slot, slot, yrs.at[3 + dy], yrr.at[((4 - dy) % 4) * 2 + 1], (apos(dy, 0), t))
    for dz in (0, 1):
        for dx in (1, 2, 3):
            slot = yl_slot(dx, dz, 0)
            arrive(slot, yls.at[0], ylr.at[dx * 4 + dz * 2])
            send(slot, slot, yls.at[8 + dz * 3 + dx], ylr.at[dx * 4 + dz * 2 + 1], (a, vpos(0, 0, 1)))
    for dz in (0, 1):
        for dy in (1, 2, 3):
            arrive(yr_slot(dy, dz), yrs.at[0], yrr.at[dy * 2 + dz])

    def turn(source, high, low, count):
        def body(j, carry):
            high_part, low_part = split(source[aligned(j, 128), :].T)
            high[:, aligned(j, 128)] = high_part
            low[:, aligned(j, 128)] = low_part
            return carry
        lax.fori_loop(0, count, body, 0)

    turn(yrbuf, yrt_h, yrt_l, 8)

    local_v.wait()
    for o in range(1, 8):
        arrive(vbuf.at[aligned(apos(o // 2, o % 2), 128), :], vs.at[o], vr.at[o])
    out_copies = [
        pltpu.make_async_copy(vbuf, v_out, osem.at[0]),
        pltpu.make_async_copy(yrbuf, yr_out, osem.at[1]),
    ]
    for copy in out_copies:
        copy.start()

    def right_tile(n, carry):
        acc[...] = jnp.zeros_like(acc)

        def step(k, carry):
            high, low = split(vbuf[aligned(k, 512), aligned(n, 256)])
            acc[...] += three(yrt_h[:, aligned(k, 512)], yrt_l[:, aligned(k, 512)], high, low)
            return carry
        lax.fori_loop(0, 2, step, 0)
        spr[aligned(n, 256), :] = acc[...].T
        return carry
    lax.fori_loop(0, 4, right_tile, 0)

    send(spr.at[aligned(1 - c, 512), :], core_in, rs.at[0], rr.at[0], (a, vpos(0, 0, 1)))

    for o in range(1, 16, 2):
        arrive(yl_slot(o // 4, (o // 2) % 2, 1), yls.at[0], ylr.at[o])
    copy = pltpu.make_async_copy(ylbuf, yl_out, osem.at[2])
    copy.start()
    out_copies.append(copy)
    turn(ylbuf, ylt_h, ylt_l, 16)

    arrive(core_in, rs.at[0], rr.at[0])
    spr[aligned(c, 512), :] += core_in[...]
    for dx in (2, 1, 3):
        send(spr.at[aligned(c * 4 + lax.rem(x + dx, 4), 128), :], x_in.at[(4 - dx) % 4 - 1],
             rs.at[dx], rr.at[(4 - dx) % 4], (a, vpos(dx, 0, 0)))
    for dx in (1, 2, 3):
        arrive(x_in.at[dx - 1], rs.at[dx], rr.at[dx])
    place = aligned(c * 4 + x, 128)
    shr[...] = spr[place, :] + x_in[0] + x_in[1] + x_in[2]
    send(shr, zl_in, rs.at[4], rr.at[4], (a, vpos(0, 1, 0)))
    arrive(zl_in, rs.at[4], rr.at[4])
    sfr[place, :] = shr[...] + zl_in[...]
    for dx in (2, 1, 3):
        send(sfr.at[place, :], sfr.at[place, :], rs.at[4 + dx], rr.at[4 + (4 - dx) % 4], (a, vpos(dx, 0, 0)))
    send(sfr.at[place, :], sfr.at[place, :], rs.at[8], rr.at[8], (a, vpos(0, 0, 1)))

    local_u.wait()

    def left_part(part):
        for offset in VERT_OFFSETS:
            arrive(ubuf.at[aligned(vpos(*offset), 128), pl.ds(part * 256, 256)],
                   us.at[part, flat(offset)], ur.at[part, flat(offset)])
        copy = pltpu.make_async_copy(
            ubuf.at[:, pl.ds(part * 256, 256)], u_out.at[:, pl.ds(part * 256, 256)], osem.at[3 + part])
        copy.start()
        out_copies.append(copy)
        acc[...] = jnp.zeros_like(acc)

        def step(k, carry):
            high, low = split(ubuf[aligned(k, 512), pl.ds(part * 256, 256)])
            acc[...] += three(ylt_h[:, aligned(k, 512)], ylt_l[:, aligned(k, 512)], high, low)
            return carry
        lax.fori_loop(0, 4, step, 0)
        spl[part] = acc[...].T
        for dy in (2, 1, 3):
            send(spl.at[part, aligned(lax.rem(y + dy, 4), 64), :], y_in.at[part, (4 - dy) % 4 - 1],
                 ls.at[part, dy], lr.at[part, (4 - dy) % 4], (apos(dy, 0), t))

    def left_reduce(part):
        for dy in (1, 2, 3):
            arrive(y_in.at[part, dy - 1], ls.at[part, dy], lr.at[part, dy])
        shl[part] = spl[part, aligned(y, 64), :] + y_in[part, 0] + y_in[part, 1] + y_in[part, 2]
        send(shl.at[part], zh_in.at[part], ls.at[part, 4], lr.at[part, 4], (apos(0, 1), t))
        arrive(zh_in.at[part], ls.at[part, 4], lr.at[part, 4])
        spot = aligned(part * 4 + y, 64)
        sfl[spot, :] = shl[part] + zh_in[part]
        for dy in (2, 1, 3):
            send(sfl.at[spot, :], sfl.at[spot, :], ls.at[part, 4 + dy], lr.at[part, 4 + (4 - dy) % 4],
                 (apos(dy, 0), t))

    left_part(0)

    for dx in (1, 2, 3):
        got = sfr.at[aligned(c * 4 + lax.rem(x + dx, 4), 128), :]
        arrive(got, rs.at[0], rr.at[4 + dx])
        send(got, got, rs.at[8 + dx], rr.at[8 + dx], (a, vpos(0, 0, 1)))

    left_reduce(0)

    for dx in (0, 1, 2, 3):
        arrive(sfr.at[aligned((1 - c) * 4 + lax.rem(x + dx, 4), 128), :], rs.at[0], rr.at[8 + dx])
    copy = pltpu.make_async_copy(sfr, sr_out, osem.at[5])
    copy.start()
    out_copies.append(copy)

    left_part(1)
    left_reduce(1)
    for part in range(2):
        for dy in (1, 2, 3):
            arrive(sfl.at[aligned(part * 4 + lax.rem(y + dy, 4), 64), :], ls.at[part, dy], lr.at[part, 4 + dy])
    copy = pltpu.make_async_copy(sfl, sl_out, osem.at[6])
    copy.start()
    out_copies.append(copy)
    for copy in sent:
        copy.wait_send()
    for copy in out_copies:
        copy.wait()


def merged(factors, grams):
    rows = [None] * 4
    for p in (3, 2, 1, 0):
        unit = (lax.broadcasted_iota(jnp.int32, (128, 512), 0) + p * 128
                == lax.broadcasted_iota(jnp.int32, (128, 512), 1)).astype(f32)
        for q in range(p + 1, 4):
            unit = unit - exact(grams[PAIRS.index((p, q))], rows[q])
        rows[p] = exact(factors[p], unit)
    return jnp.concatenate(rows, axis=0)


def update_kernel(tl, tr, grams, sl, sr, yl, u, yr, v, u_out, v_out, wl_h, wl_l, wr_h, wr_l):
    step = pl.program_id(0)
    upper = (lax.broadcasted_iota(jnp.int32, (128, 128), 0)
             <= lax.broadcasted_iota(jnp.int32, (128, 128), 1))

    @pl.when(step == 0)
    def _():
        factors = [jnp.where(upper, tl[p], 0.0) for p in range(4)]
        total = merged(factors, [grams[i] for i in range(6)])
        high, low = split(total)
        s_high, s_low = split(sl[...])
        wl_h[...], wl_l[...] = split(three(high, low, s_high, s_low, dot_t))
        factors = [jnp.where(upper, tr[p], 0.0).T for p in range(4)]
        total = merged(factors, [grams[6 + i] for i in range(6)])
        high, low = split(total)
        s_high, s_low = split(sr[...])
        wr_h[...], wr_l[...] = split(three(high, low, s_high, s_low, dot_t))

    @pl.when(step < 4)
    def _():
        high, low = split(yl[...])
        u_out[...] = u[...] - three(high, low, wl_h[...], wl_l[...])

    @pl.when(step >= 4)
    def _():
        high, low = split(yr[...])
        v_out[...] = v[...] - three(high, low, wr_h[...], wr_l[...])


def shards(u_band, v_band, y_left, t_left, y_right, t_right):
    any_space = pl.BlockSpec(memory_space=pl.ANY)
    vmem = pl.BlockSpec(memory_space=pltpu.VMEM)
    shape = jax.ShapeDtypeStruct
    grams = pl.pallas_call(
        gram_kernel,
        out_shape=shape((12, 128, 128), f32),
        in_specs=[vmem, vmem],
        out_specs=vmem,
    )(y_left, y_right)
    grams = lax.psum(grams, ("au", "vert"))

    dma = pltpu.SemaphoreType.DMA
    buf = lambda *dims: pltpu.VMEM(dims, f32)
    half = lambda *dims: pltpu.VMEM(dims, bf16)
    u_all, v_all, yl_all, yr_all, s_left, s_right = pl.pallas_call(
        move_kernel,
        out_shape=[
            shape((2048, 512), f32), shape((1024, 1024), f32),
            shape((2048, 512), f32), shape((1024, 512), f32),
            shape((512, 512), f32), shape((1024, 512), f32),
        ],
        in_specs=[any_space] * 4,
        out_specs=[any_space] * 6,
        scratch_shapes=[
            buf(2048, 512), buf(1024, 1024), buf(2048, 512), buf(1024, 512),
            half(512, 2048), half(512, 2048), half(512, 1024), half(512, 1024), buf(512, 256),
            buf(1024, 512), buf(512, 512), buf(3, 128, 512), buf(128, 512), buf(128, 512), buf(1024, 512),
            buf(2, 256, 512), buf(2, 3, 64, 512), buf(2, 64, 512), buf(2, 64, 512), buf(512, 512),
            dma((10,)), dma((8,)), dma((16,)), dma((16,)), dma((8,)), dma((8,)),
            dma((2, 16)), dma((2, 16)), dma((8,)), dma((8,)),
            dma((12,)), dma((12,)), dma((2, 8)), dma((2, 8)),
        ],
        compiler_params=pltpu.CompilerParams(
            collective_id=0, has_side_effects=True, vmem_limit_bytes=48 * 2**20,
        ),
        cost_estimate=pl.CostEstimate(flops=2 * 10**10, bytes_accessed=4 * 10**8, transcendentals=0),
    )(y_left, y_right, u_band, v_band)

    first = lambda i: (jnp.minimum(i, 3), 0)
    second = lambda i: (jnp.maximum(i - 4, 0), 0)
    whole2 = lambda i: (0, 0)
    whole3 = lambda i: (0, 0, 0)
    return pl.pallas_call(
        update_kernel,
        grid=(8,),
        out_shape=[shape((2048, 512), f32), shape((1024, 1024), f32)],
        in_specs=[
            pl.BlockSpec((4, 128, 128), whole3), pl.BlockSpec((4, 128, 128), whole3),
            pl.BlockSpec((12, 128, 128), whole3),
            pl.BlockSpec((512, 512), whole2), pl.BlockSpec((1024, 512), whole2),
            pl.BlockSpec((512, 512), first), pl.BlockSpec((512, 512), first),
            pl.BlockSpec((256, 512), second), pl.BlockSpec((256, 1024), second),
        ],
        out_specs=[pl.BlockSpec((512, 512), first), pl.BlockSpec((256, 1024), second)],
        scratch_shapes=[half(512, 512), half(512, 512), half(512, 1024), half(512, 1024)],
        compiler_params=pltpu.CompilerParams(vmem_limit_bytes=48 * 2**20),
    )(t_left, t_right, grams, s_left, s_right, yl_all, u_all, yr_all, v_all)


def solution(mesh):
    return jax.shard_map(
        shards,
        mesh=mesh,
        in_specs=(
            P(("au", "vert"), None),
            P(("vert", "au"), None),
            P(None, ("au", "vert"), None),
            P(),
            P(None, ("vert", "au"), None),
            P(),
        ),
        out_specs=(P("au", "vert"), P("vert", "au")),
        check_vma=False,
    )
```

time: 477 us -> 271 us (0.57); the launches traced: 472 us -> 271 us
  Pallas kernels: 0 us -> 205 us
  waiting for transfers between devices: 192 us -> 46.6 us
  starting transfers between devices: 122 us -> 0.04 us
  matrix products: 95.7 us -> 0 us
  local copies, waits for them, and re-layouts: 47.4 us -> 5.3 us
    pallas_call x0 -> x3, Pallas kernels: none -> 205 us  [the longest x1 180 us: shards(): pl.pallas_call(move_kernel, out_shape=[shape((2048, 512), f32), shape((10...]
    all_to_all x19 -> x0, waiting for transfers between devices: 191 us -> none  [the longest x1 56.6 us: shards(): lax.all_to_all(v_band, 'au', split_axis=1, concat_axis=0, tiled=True)]
    all_to_all x19 -> x0, starting transfers between devices: 122 us -> none  [the longest x8 63.6 us: sent_and_summed(): lax.all_to_all(parts, axis, split_axis=0, concat_axis=0, tiled=True)]
    dot_general x24 -> x0, matrix products: 95.7 us -> none  [the longest x16 51.6 us: product(): jnp.dot(left, right, precision=highest, preferred_element_type=jnp.float32)]
    psum x0 -> x1, waiting for transfers between devices: none -> 46.6 us  [shards(): grams = lax.psum(grams, ('au', 'vert'))]
    unnamed x20 -> x12, local copies, waits for them, and re-layouts: 29.9 us -> 5.3 us
    broadcast_in_dim x9 -> x0, local copies, waits for them, and re-layouts: 8.8 us -> none  [from_everyone(): jnp.broadcast_to(value[None], (length, *value.shape))]
    all_to_all x2 -> x0, local copies, waits for them, and re-layouts: 7.6 us -> none  [the longest x1 4.76 us: shards(): lax.all_to_all(u_band, 'vert', split_axis=1, concat_axis=0, tiled=True)]
  transfers between devices with their start and end apart: 20 -> 1, of which waited for: 15 -> 1; matrix products, arithmetic and copies ran while one was open for 22% -> 0% of each run, Pallas kernels for 0% -> 66%
where the time goes in v1:
time: 271 us
  Pallas kernels  205 us (76%)
  waiting for transfers between devices  46.6 us (17%)
  between operations  14.1 us (5%)
  local copies, waits for them, and re-layouts  5.3 us (2%)
    pallas_call x1, Pallas kernels, shards(): pl.pallas_call(move_kernel, out_shape=[shape((2048, 512), f32), shape((10...  180 us
    psum x1, waiting for transfers between devices, shards(): grams = lax.psum(grams, ('au', 'vert'))  46.6 us
    pallas_call x1, Pallas kernels, shards(): pl.pallas_call(update_kernel, grid=(8,), out_shape=[shape((2048, 512), f3...  21.9 us
  transfers between devices with their start and end apart: 1, of which 1 were waited for; matrix products, arithmetic and copies ran while one was open for 0% of the time, Pallas kernels for 66%

profile of v1, /device:TPU:1, one launch (start us, length us, event | category | flops | bytes accessed | tf_op | source)
XLA Modules:
  0.0 270.7 jit_solution(2707614810074497670)
XLA Ops:
  7.2 0.0 all-reduce.2.cloned.1.call-start
  7.2 2.8 %shard_map.77 = f32[12,128,128]{2,1,0:T(8,128)} custom-call(f32[4,128,128]{2,1,0:T(8,128)} %yl.3, f32[4,128,128]{2,1,0:T(8,128)} %yr.3), custom_call_target="tpu_custom_call" | custom-call | tf_op jit(solution)/shard_map/pallas_call | solution.py:325
  10.0 0.0 all-reduce.2.cloned.1.call-update
  10.0 0.0 copy-start.4
  10.0 0.9 copy-done.4
  11.0 0.0 copy-start.5
  11.0 0.9 copy-done.5
  11.9 0.0 copy-start.2
  11.9 180.0 %shard_map.78 = (f32[2048,512]{1,0:T(8,128)}, f32[1024,1024]{1,0:T(8,128)}, f32[2048,512]{1,0:T(8,128)}, f32[1024,512]{1,0:T(8,128)S(1)}, f32[512,512]{1,0:T(8,128)S(1)}, /*index=5*/f32[1024,512]{1,0:T(8,128)S(1)}) custom-call(f32[4,128,128]{2,1,0:T(8,128)S(1)} %copy-done.4, f32[4,128,128]{2,1,0:T(8,128)S(1)} %copy-done.5, f32[128,8192]{1,0:T(8,128)} %u.1, ...), custom_call_target="tpu_custom_call" | custom-call | flops 20000000000 | bytes 400000000 | tf_op jit(solution)/shard_map/pallas_call | solution.py:336
  191.9 0.0 copy-start
  192.0 1.3 copy-done
  193.3 46.6 %all-reduce.2.cloned.1.call-done.grams = f32[12,128,128]{2,1,0:T(8,128)} async-done(((f32[12,128,128]{2,1,0:T(8,128)}), f32[12,128,128]{2,1,0:T(8,128)}) %all-reduce.2.cloned.1.call-update) | async-done | bytes 786448 | tf_op jit(solution)/shard_map/psum | solution.py:331
  239.9 0.0 copy-done.2
  239.9 0.0 copy-start.1
  239.9 1.1 copy-done.1
  241.0 0.0 copy-start.3
  241.0 0.9 copy-done.3
  242.0 21.9 %shard_map.79 = (f32[2048,512]{1,0:T(8,128)}, f32[1024,1024]{1,0:T(8,128)}) custom-call(f32[4,128,128]{2,1,0:T(8,128)S(1)} %copy-done.2, f32[4,128,128]{2,1,0:T(8,128)S(1)} %copy-done.3, f32[12,128,128]{2,1,0:T(8,128)S(1)} %copy-done.1, f32[512,512]{1,0:T(8,128)S(1)} %get-tuple-element.8.sl, f32[1024,512]{1,0:T(8,128)S(1)} %get-tuple-element.9.sr, ...), custom_call_target="tpu_custom_call" | custom-call | tf_op jit(solution)/shard_map/pallas_call | solution.py:364
Async XLA Ops:
  7.2 232.7 %all-reduce.2.cloned.1.call-start = ((), (), s32[]{:S(2)}) async-start(), calls=%async_computation | async-start | bytes 1572864 | tf_op jit(solution)/shard_map/psum | solution.py:331
  10.0 1.0 copy-start.4
  11.0 0.9 copy-start.5
  11.9 228.0 %copy-start.2 = (f32[4,128,128]{2,1,0:T(8,128)S(1)}, f32[4,128,128]{2,1,0:T(8,128)}, u32[]{:S(2)}) copy-start(f32[4,128,128]{2,1,0:T(8,128)} %tl.1) | copy-start | bytes 786436
  191.9 1.3 copy-start
  239.9 1.1 copy-start.1
  241.0 0.9 copy-start.3
Sparse Core Ops, SparseCore 0:
  13.2 226.6 all-reduce.1

commit v2 on v1

v2 whole, which is shorter than its diff:
```python
import functools

import jax
import jax.numpy as jnp
from jax import lax
from jax.experimental import pallas as pl
from jax.experimental.pallas import tpu as pltpu
from jax.sharding import PartitionSpec as P

MESH = pl.DeviceIdType.MESH
f32 = jnp.float32
bf16 = jnp.bfloat16
PARTS = (256, 256)
STARTS = [sum(PARTS[:part]) for part in range(len(PARTS))]
PAIRS = [(0, 1), (0, 2), (0, 3), (1, 2), (1, 3), (2, 3)]
VERT_OFFSETS = [(dx, dz, dc) for dx in (2, 1, 3, 0) for dz in (1, 0) for dc in (0, 1)][:-2] + [(0, 0, 1)]


def split(value):
    high = value.astype(bf16)
    return high, (value - high.astype(f32)).astype(bf16)


def dot(a, b):
    return lax.dot_general(a, b, (((1,), (0,)), ((), ())), preferred_element_type=f32)


def dot_t(a, b):
    return lax.dot_general(a, b, (((1,), (1,)), ((), ())), preferred_element_type=f32)


def three(a_high, a_low, b_high, b_low, product=dot):
    return product(a_high, b_high) + product(a_high, b_low) + product(a_low, b_high)


def exact(a, b):
    return jnp.dot(a, b, precision=lax.Precision.HIGHEST, preferred_element_type=f32)


def aligned(index, size):
    return pl.ds(pl.multiple_of(index * size, size), size)


def flat(offset):
    dx, dz, dc = offset
    return dx * 4 + dz * 2 + dc


def back(offset):
    dx, dz, dc = offset
    return ((4 - dx) % 4, dz, dc)


def merged(factors, grams):
    rows = [None] * 4
    for p in (3, 2, 1, 0):
        unit = (lax.broadcasted_iota(jnp.int32, (128, 512), 0) + p * 128
                == lax.broadcasted_iota(jnp.int32, (128, 512), 1)).astype(f32)
        for q in range(p + 1, 4):
            unit = unit - exact(grams[PAIRS.index((p, q))], rows[q])
        rows[p] = exact(factors[p], unit)
    return jnp.concatenate(rows, axis=0)


def upper(t):
    keep = (lax.broadcasted_iota(jnp.int32, (128, 128), 0)
            <= lax.broadcasted_iota(jnp.int32, (128, 128), 1))
    return jnp.where(keep, t, 0.0)


def move_kernel(
    yl, yr, u, v, tl_in, tr_in,
    u_out, v_out, yl_out, yr_out, wl_out, wr_out,
    ubuf, vbuf, ylbuf, yrbuf, ylt_h, ylt_l, yrt_h, yrt_l,
    spr, core_in, x_in, shr, zl_in, wr,
    spl, y_in, shl, zh_in, wl,
    gl, gl_in, gl_sh, gl_z, gl_all, gr, gr_core, gr_sum, gr_in, gr_sh, gr_z, gr_all,
    tl_h, tl_l, tr_h, tr_l, tl, tr,
    lsem, osem, yls, ylr, yrs, yrr, us, ur, vs, vr,
    rs, rr, ls, lr, gls, glr, grs, grr,
):
    a = lax.axis_index("au")
    t = lax.axis_index("vert")
    y, zh = a // 2, a % 2
    x, zl, c = t // 4, (t // 2) % 2, t % 2

    def vpos(dx, dz, dc):
        return lax.rem(x + dx, 4) * 4 + lax.rem(zl + dz, 2) * 2 + lax.rem(c + dc, 2)

    def apos(dy, dz):
        return lax.rem(y + dy, 4) * 2 + lax.rem(zh + dz, 2)

    sent = []

    def send(src, dst, ssem, rsem, device):
        copy = pltpu.make_async_remote_copy(
            src_ref=src, dst_ref=dst, send_sem=ssem, recv_sem=rsem,
            device_id=device, device_id_type=MESH,
        )
        copy.start()
        sent.append(copy)

    def arrive(dst, sem):
        pltpu.make_async_remote_copy(
            src_ref=dst, dst_ref=dst, send_sem=sem, recv_sem=sem,
            device_id=(a, t), device_id_type=MESH,
        ).wait_recv()

    out_copies = []

    def put(src, dst, sem):
        copy = pltpu.make_async_copy(src, dst, sem)
        copy.start()
        out_copies.append(copy)

    locals_y = []
    for p in range(4):
        locals_y.append(pltpu.make_async_copy(
            yl.at[p], ylbuf.at[aligned(t, 128), pl.ds(p * 128, 128)], lsem.at[p]))
        locals_y.append(pltpu.make_async_copy(
            yr.at[p], yrbuf.at[aligned(a, 128), pl.ds(p * 128, 128)], lsem.at[4 + p]))
    local_u = pltpu.make_async_copy(u.at[:, aligned(t, 512)], ubuf.at[aligned(t, 128), :], lsem.at[8])
    local_v = pltpu.make_async_copy(v.at[:, aligned(a, 1024)], vbuf.at[aligned(a, 128), :], lsem.at[9])
    local_t = [pltpu.make_async_copy(tl_in, tl, lsem.at[10]), pltpu.make_async_copy(tr_in, tr, lsem.at[11])]
    for copy in locals_y + [local_u, local_v] + local_t:
        copy.start()

    barrier = pltpu.get_barrier_semaphore()
    for offset in VERT_OFFSETS:
        pl.semaphore_signal(barrier, inc=1, device_id=(a, vpos(*offset)), device_id_type=MESH)
    for o in range(1, 8):
        pl.semaphore_signal(barrier, inc=1, device_id=(apos(o // 2, o % 2), t), device_id_type=MESH)
    pl.semaphore_wait(barrier, 22)

    for copy in locals_y:
        copy.wait()

    def yl_slot(dx, dz, dc):
        return ylbuf.at[aligned(vpos(dx, dz, dc), 128), :]

    def yr_slot(dy, dz):
        return yrbuf.at[aligned(apos(dy, dz), 128), :]

    def send_v(part, o):
        dy, dz = o // 2, o % 2
        target = apos(dy, dz)
        begin, width = 2 * STARTS[part], 2 * PARTS[part]
        send(v.at[:, pl.ds(pl.multiple_of(target * 1024 + begin, 256), width)],
             vbuf.at[aligned(a, 128), pl.ds(begin, width)],
             vs.at[part, o], vr.at[part, ((4 - dy) % 4) * 2 + dz], (target, t))

    def send_u(part, offset):
        target = vpos(*offset)
        begin, width = STARTS[part], PARTS[part]
        send(u.at[:, pl.ds(pl.multiple_of(target * 512 + begin, 128), width)],
             ubuf.at[aligned(t, 128), pl.ds(begin, width)],
             us.at[part, flat(offset)], ur.at[part, flat(back(offset))], (a, target))

    def in_plane(part):
        for o in (2, 6, 4):
            send_v(part, o)
        for dc in (0, 1):
            for dx in (1, 3, 2):
                send_u(part, (dx, 0, dc))
        send_u(part, (0, 0, 1))

    def across(part):
        for o, dx in ((1, 0), (3, 1), (7, 3), (5, 2)):
            send_v(part, o)
            for dc in (0, 1):
                send_u(part, (dx, 1, dc))

    own = yl_slot(0, 0, 0)
    mine = yr_slot(0, 0)
    send(own, own, yls.at[0], ylr.at[2], (a, vpos(0, 1, 0)))
    send(mine, mine, yrs.at[0], yrr.at[1], (apos(0, 1), t))
    for d in (1, 3, 2):
        send(own, own, yls.at[d], ylr.at[((4 - d) % 4) * 4], (a, vpos(d, 0, 0)))
        send(mine, mine, yrs.at[d], yrr.at[((4 - d) % 4) * 2], (apos(d, 0), t))
    send(own, own, yls.at[7], ylr.at[1], (a, vpos(0, 0, 1)))

    slot = yl_slot(0, 1, 0)
    arrive(slot, ylr.at[2])
    for dx in (1, 3, 2):
        send(slot, slot, yls.at[3 + dx], ylr.at[((4 - dx) % 4) * 4 + 2], (a, vpos(dx, 0, 0)))
    send(slot, slot, yls.at[8], ylr.at[3], (a, vpos(0, 0, 1)))
    slot = yr_slot(0, 1)
    arrive(slot, yrr.at[1])
    for dy in (1, 3, 2):
        send(slot, slot, yrs.at[3 + dy], yrr.at[((4 - dy) % 4) * 2 + 1], (apos(dy, 0), t))

    across(0)
    in_plane(0)
    for dz in (0, 1):
        for dx in (1, 3, 2):
            slot = yl_slot(dx, dz, 0)
            arrive(slot, ylr.at[dx * 4 + dz * 2])
            send(slot, slot, yls.at[8 + dz * 3 + dx], ylr.at[dx * 4 + dz * 2 + 1], (a, vpos(0, 0, 1)))

    def turn(source, high, low, count):
        def body(j, carry):
            high_part, low_part = split(source[aligned(j, 128), :].T)
            high[:, aligned(j, 128)] = high_part
            low[:, aligned(j, 128)] = low_part
            return carry
        lax.fori_loop(0, count, body, 0)

    def gram(high, low, out):
        def block(p, n, q, m):
            rows, cols = pl.ds(p * 128, n * 128), pl.ds(q * 128, m * 128)
            return three(high[rows, :], low[rows, :], high[cols, :], low[cols, :], dot_t)
        out[0:128, :] = block(0, 1, 1, 1)
        square = block(0, 2, 2, 2)
        out[128:256, :] = square[:128, :128]
        out[256:384, :] = square[:128, 128:]
        out[384:512, :] = square[128:, :128]
        out[512:640, :] = square[128:, 128:]
        out[640:768, :] = block(2, 1, 3, 1)

    def gram_left():
        for dy in (1, 3, 2):
            send(gl.at[aligned(lax.rem(y + dy, 4), 192), :], gl_in.at[(4 - dy) % 4 - 1],
                 gls.at[dy], glr.at[(4 - dy) % 4], (apos(dy, 0), t))

    def gram_right():
        arrive(gr_core, grr.at[0])
        gr_sum[...] = gr[...] + gr_core[...]
        for dx in (1, 3, 2):
            send(gr_sum.at[aligned(lax.rem(x + dx, 4), 192), :], gr_in.at[(4 - dx) % 4 - 1],
                 grs.at[dx], grr.at[(4 - dx) % 4], (a, vpos(dx, 0, 0)))

    def gram_pair_left():
        for dy in (1, 3, 2):
            arrive(gl_in.at[dy - 1], glr.at[dy])
        gl_sh[...] = gl[aligned(y, 192), :] + gl_in[0] + gl_in[1] + gl_in[2]
        send(gl_sh, gl_z, gls.at[4], glr.at[4], (apos(0, 1), t))

    def gram_pair_right():
        for dx in (1, 3, 2):
            arrive(gr_in.at[dx - 1], grr.at[dx])
        gr_sh[...] = gr_sum[aligned(x, 192), :] + gr_in[0] + gr_in[1] + gr_in[2]
        send(gr_sh, gr_z, grs.at[4], grr.at[4], (a, vpos(0, 1, 0)))

    def gram_spread_left():
        arrive(gl_z, glr.at[4])
        spot_l = gl_all.at[aligned(y, 192), :]
        spot_l[...] = gl_sh[...] + gl_z[...]
        for dy in (1, 3, 2):
            send(spot_l, spot_l, gls.at[4 + dy], glr.at[4 + (4 - dy) % 4], (apos(dy, 0), t))

    def gram_spread_right():
        arrive(gr_z, grr.at[4])
        spot_r = gr_all.at[aligned(x, 192), :]
        spot_r[...] = gr_sh[...] + gr_z[...]
        for dx in (1, 3, 2):
            send(spot_r, spot_r, grs.at[4 + dx], grr.at[4 + (4 - dx) % 4], (a, vpos(dx, 0, 0)))

    def merge_left():
        for dy in (1, 2, 3):
            arrive(gl_all.at[aligned(lax.rem(y + dy, 4), 192), :], glr.at[4 + dy])
        tl_h[...], tl_l[...] = split(merged(
            [upper(tl[p]) for p in range(4)], [gl_all[pl.ds(i * 128, 128), :] for i in range(6)]))

    def merge_right():
        for dx in (1, 2, 3):
            arrive(gr_all.at[aligned(lax.rem(x + dx, 4), 192), :], grr.at[4 + dx])
        tr_h[...], tr_l[...] = split(merged(
            [upper(tr[p]).T for p in range(4)], [gr_all[pl.ds(i * 128, 128), :] for i in range(6)]))

    for o in range(1, 16, 2):
        arrive(yl_slot(o // 4, (o // 2) % 2, 1), ylr.at[o])
    put(ylbuf, yl_out, osem.at[1])
    turn(ylbuf, ylt_h, ylt_l, 16)
    gram(ylt_h, ylt_l, gl)
    gram_left()

    for dz in (0, 1):
        for dy in (1, 3, 2):
            arrive(yr_slot(dy, dz), yrr.at[dy * 2 + dz])
    put(yrbuf, yr_out, osem.at[0])
    turn(yrbuf, yrt_h, yrt_l, 8)
    gram(yrt_h, yrt_l, gr)
    send(gr, gr_core, grs.at[0], grr.at[0], (a, vpos(0, 0, 1)))

    gram_right()
    across(1)
    in_plane(1)
    for copy in local_t + [local_u, local_v]:
        copy.wait()
    def right_sums(part):
        begin, width = 2 * STARTS[part], 2 * PARTS[part]
        for o in range(1, 8):
            arrive(vbuf.at[aligned(apos(o // 2, o % 2), 128), pl.ds(begin, width)], vr.at[part, o])
        put(vbuf.at[:, pl.ds(begin, width)], v_out.at[:, pl.ds(begin, width)], osem.at[2 + part])

        def tile(n, carry):
            columns = pl.ds(pl.multiple_of(begin + n * 256, 256), 256)
            high, low = split(vbuf[:, columns])
            spr[columns, :] = three(yrt_h[...], yrt_l[...], high, low).T
            return carry
        lax.fori_loop(0, width // 256, tile, 0)
        half = PARTS[part]
        send(spr.at[pl.ds(pl.multiple_of(begin + (1 - c) * half, 128), half), :],
             core_in.at[pl.ds(STARTS[part], half), :], rs.at[part, 0], rr.at[part, 0], (a, vpos(0, 0, 1)))

    def right_share(part, core, row):
        half = PARTS[part]
        return pl.ds(pl.multiple_of(2 * STARTS[part] + core * half + row * (half // 4), 32), half // 4)

    def left_share(part, row):
        quarter = PARTS[part] // 4
        return pl.ds(pl.multiple_of(STARTS[part] + row * quarter, 32), quarter)

    def inner(part):
        return pl.ds(STARTS[part] // 4, PARTS[part] // 4)

    def right_core(part):
        half = PARTS[part]
        arrive(core_in.at[pl.ds(STARTS[part], half), :], rr.at[part, 0])
        mine = pl.ds(pl.multiple_of(2 * STARTS[part] + c * half, 128), half)
        spr[mine, :] += core_in[pl.ds(STARTS[part], half), :]
        for dx in (1, 3, 2):
            send(spr.at[right_share(part, c, lax.rem(x + dx, 4)), :], x_in.at[(4 - dx) % 4 - 1, inner(part), :],
                 rs.at[part, dx], rr.at[part, (4 - dx) % 4], (a, vpos(dx, 0, 0)))

    def right_pair(part):
        for dx in (1, 2, 3):
            arrive(x_in.at[dx - 1, inner(part), :], rr.at[part, dx])
        at = inner(part)
        shr[at, :] = spr[right_share(part, c, x), :] + x_in[0, at, :] + x_in[1, at, :] + x_in[2, at, :]
        send(shr.at[at, :], zl_in.at[at, :], rs.at[part, 4], rr.at[part, 4], (a, vpos(0, 1, 0)))

    def right_spread(part):
        at = inner(part)
        arrive(zl_in.at[at, :], rr.at[part, 4])
        high, low = split(shr[at, :] + zl_in[at, :])
        place = wr.at[right_share(part, c, x), :]
        place[...] = three(high, low, tr_h[...], tr_l[...], dot_t)
        for dx in (1, 3, 2):
            send(place, place, rs.at[part, 4 + dx], rr.at[part, 4 + (4 - dx) % 4], (a, vpos(dx, 0, 0)))
        send(place, place, rs.at[part, 8], rr.at[part, 8], (a, vpos(0, 0, 1)))

    def right_onward(part):
        for dx in (1, 3, 2):
            got = wr.at[right_share(part, c, lax.rem(x + dx, 4)), :]
            arrive(got, rr.at[part, 4 + dx])
            send(got, got, rs.at[part, 8 + dx], rr.at[part, 8 + dx], (a, vpos(0, 0, 1)))

    def right_done(part):
        for dx in (0, 1, 2, 3):
            arrive(wr.at[right_share(part, 1 - c, lax.rem(x + dx, 4)), :], rr.at[part, 8 + dx])

    def left_sums(part):
        begin, width = STARTS[part], PARTS[part]
        for offset in VERT_OFFSETS:
            arrive(ubuf.at[aligned(vpos(*offset), 128), pl.ds(begin, width)], ur.at[part, flat(offset)])
        put(ubuf.at[:, pl.ds(begin, width)], u_out.at[:, pl.ds(begin, width)], osem.at[4 + part])
        for tile in range(begin, begin + width, 256):
            columns = pl.ds(tile, min(256, begin + width - tile))
            high, low = split(ubuf[:, columns])
            spl[columns, :] = three(ylt_h[...], ylt_l[...], high, low).T
        for dy in (1, 3, 2):
            send(spl.at[left_share(part, lax.rem(y + dy, 4)), :], y_in.at[(4 - dy) % 4 - 1, inner(part), :],
                 ls.at[part, dy], lr.at[part, (4 - dy) % 4], (apos(dy, 0), t))

    def left_pair(part):
        at = inner(part)
        for dy in (1, 2, 3):
            arrive(y_in.at[dy - 1, at, :], lr.at[part, dy])
        shl[at, :] = spl[left_share(part, y), :] + y_in[0, at, :] + y_in[1, at, :] + y_in[2, at, :]
        send(shl.at[at, :], zh_in.at[at, :], ls.at[part, 4], lr.at[part, 4], (apos(0, 1), t))

    def left_spread(part):
        at = inner(part)
        arrive(zh_in.at[at, :], lr.at[part, 4])
        high, low = split(shl[at, :] + zh_in[at, :])
        place = wl.at[left_share(part, y), :]
        place[...] = three(high, low, tl_h[...], tl_l[...], dot_t)
        for dy in (1, 3, 2):
            send(place, place, ls.at[part, 4 + dy], lr.at[part, 4 + (4 - dy) % 4], (apos(dy, 0), t))

    def left_done(part):
        for dy in (1, 2, 3):
            arrive(wl.at[left_share(part, lax.rem(y + dy, 4)), :], lr.at[part, 4 + dy])

    right_sums(0)
    left_sums(0)
    right_core(0)
    gram_pair_right()
    gram_pair_left()
    left_pair(0)
    right_pair(0)
    gram_spread_right()
    gram_spread_left()
    right_sums(1)
    left_sums(1)
    right_core(1)
    merge_right()
    merge_left()
    left_spread(0)
    right_spread(0)
    left_pair(1)
    right_pair(1)
    right_onward(0)
    left_spread(1)
    right_spread(1)
    right_onward(1)
    for part in range(2):
        left_done(part)
        right_done(part)
    put(wr, wr_out, osem.at[6])
    put(wl, wl_out, osem.at[7])
    for copy in sent:
        copy.wait_send()
    for copy in out_copies:
        copy.wait()


def update_kernel(wl, yl, u, yr, v, wr, u_out, v_out, wl_h, wl_l, wr_h, wr_l):
    step = pl.program_id(0)

    @pl.when(step == 0)
    def _():
        wl_h[...], wl_l[...] = split(wl[...])

    @pl.when(step == 4)
    def _():
        wr_h[...], wr_l[...] = split(wr[...])

    @pl.when(step < 4)
    def _():
        high, low = split(yl[...])
        u_out[...] = u[...] - three(high, low, wl_h[...], wl_l[...], dot_t)

    @pl.when(step >= 4)
    def _():
        high, low = split(yr[...])
        v_out[...] = v[...] - three(high, low, wr_h[...], wr_l[...], dot_t)


def shards(u_band, v_band, y_left, t_left, y_right, t_right):
    any_space = pl.BlockSpec(memory_space=pl.ANY)
    shape = jax.ShapeDtypeStruct
    dma = pltpu.SemaphoreType.DMA
    buf = lambda *dims: pltpu.VMEM(dims, f32)
    half = lambda *dims: pltpu.VMEM(dims, bf16)
    u_all, v_all, yl_all, yr_all, w_left, w_right = pl.pallas_call(
        move_kernel,
        out_shape=[
            shape((2048, 512), f32), shape((1024, 1024), f32),
            shape((2048, 512), f32), shape((1024, 512), f32),
            shape((512, 512), f32), shape((1024, 512), f32),
        ],
        in_specs=[any_space] * 6,
        out_specs=[any_space] * 6,
        scratch_shapes=[
            buf(2048, 512), buf(1024, 1024), buf(2048, 512), buf(1024, 512),
            half(512, 2048), half(512, 2048), half(512, 1024), half(512, 1024),
            buf(1024, 512), buf(512, 512), buf(3, 128, 512), buf(128, 512), buf(128, 512), buf(1024, 512),
            buf(512, 512), buf(3, 128, 512), buf(128, 512), buf(128, 512), buf(512, 512),
            buf(768, 128), buf(3, 192, 128), buf(192, 128), buf(192, 128), buf(768, 128),
            buf(768, 128), buf(768, 128), buf(768, 128), buf(3, 192, 128), buf(192, 128), buf(192, 128), buf(768, 128),
            half(512, 512), half(512, 512), half(512, 512), half(512, 512),
            buf(4, 128, 128), buf(4, 128, 128),
            dma((12,)), dma((8,)), dma((16,)), dma((16,)), dma((8,)), dma((8,)),
            dma((len(PARTS), 16)), dma((len(PARTS), 16)), dma((len(PARTS), 8)), dma((len(PARTS), 8)),
            dma((len(PARTS), 12)), dma((len(PARTS), 12)), dma((len(PARTS), 8)), dma((len(PARTS), 8)),
            dma((8,)), dma((8,)), dma((8,)), dma((8,)),
        ],
        compiler_params=pltpu.CompilerParams(
            collective_id=0, has_side_effects=True, vmem_limit_bytes=60 * 2**20,
        ),
        cost_estimate=pl.CostEstimate(flops=2 * 10**10, bytes_accessed=4 * 10**8, transcendentals=0),
    )(y_left, y_right, u_band, v_band, t_left, t_right)

    first = lambda i: (jnp.minimum(i, 3), 0)
    second = lambda i: (jnp.maximum(i - 4, 0), 0)
    whole = lambda i: (0, 0)
    return pl.pallas_call(
        update_kernel,
        grid=(8,),
        out_shape=[shape((2048, 512), f32), shape((1024, 1024), f32)],
        in_specs=[
            pl.BlockSpec((512, 512), whole),
            pl.BlockSpec((512, 512), first), pl.BlockSpec((512, 512), first),
            pl.BlockSpec((256, 512), second), pl.BlockSpec((256, 1024), second),
            pl.BlockSpec((1024, 512), whole),
        ],
        out_specs=[pl.BlockSpec((512, 512), first), pl.BlockSpec((256, 1024), second)],
        scratch_shapes=[half(512, 512), half(512, 512), half(1024, 512), half(1024, 512)],
        compiler_params=pltpu.CompilerParams(vmem_limit_bytes=48 * 2**20),
    )(w_left, yl_all, u_all, yr_all, v_all, w_right)


def solution(mesh):
    return jax.shard_map(
        shards,
        mesh=mesh,
        in_specs=(
            P(("au", "vert"), None),
            P(("vert", "au"), None),
            P(None, ("au", "vert"), None),
            P(),
            P(None, ("vert", "au"), None),
            P(),
        ),
        out_specs=(P("au", "vert"), P("vert", "au")),
        check_vma=False,
    )
```

time: 271 us -> 174 us (0.64)
  waiting for transfers between devices: 46.6 us -> 0 us
  Pallas kernels: 205 us -> 168 us
  between operations: 14.1 us -> 0.65 us
    psum x1 -> x0, waiting for transfers between devices: 46.6 us -> none  [shards(): grams = lax.psum(grams, ('au', 'vert'))]
    pallas_call x1, Pallas kernels: 180 us -> 154 us  [shards(): pl.pallas_call(move_kernel, out_shape=[shape((2048, 512), f32), shape((10...]
    pallas_call x1, Pallas kernels: 21.9 us -> 13.7 us  [shards(): pl.pallas_call(update_kernel, grid=(8,), out_shape=[shape((2048, 512), f3...]
    pallas_call x1 -> x0, Pallas kernels: 2.79 us -> none  [shards(): pl.pallas_call(gram_kernel, out_shape=shape((12, 128, 128), f32), in_spec...]
  transfers between devices with their start and end apart: 1 -> 0, of which waited for: 1 -> 0; matrix products, arithmetic and copies ran while one was open for 0% -> 0% of each run, Pallas kernels for 66% -> 0%
where the time goes in v2:
time: 174 us; the launch traced here: 173 us
  Pallas kernels  168 us (97%)
  local copies, waits for them, and re-layouts  4.4 us (3%)
    pallas_call x1, Pallas kernels, shards(): pl.pallas_call(move_kernel, out_shape=[shape((2048, 512), f32), shape((10...  154 us
    pallas_call x1, Pallas kernels, shards(): pl.pallas_call(update_kernel, grid=(8,), out_shape=[shape((2048, 512), f3...  13.7 us
    unnamed x6, local copies, waits for them, and re-layouts  4.4 us

profile of v2, /device:TPU:1, one launch (start us, length us, event | category | flops | bytes accessed | tf_op | source)
XLA Modules:
  0.0 173.2 jit_solution(6902026243375544577)
XLA Ops:
  0.6 154.5 %shard_map.77 = (f32[2048,512]{1,0:T(8,128)}, f32[1024,1024]{1,0:T(8,128)}, f32[2048,512]{1,0:T(8,128)}, f32[1024,512]{1,0:T(8,128)}, f32[512,512]{1,0:T(8,128)}, /*index=5*/f32[1024,512]{1,0:T(8,128)}) custom-call(f32[4,128,128]{2,1,0:T(8,128)} %yl.1, f32[4,128,128]{2,1,0:T(8,128)} %yr.1, f32[128,8192]{1,0:T(8,128)} %u.1, f32[128,8192]{1,0:T(8,128)} %v.1, ...), custom_call_target="tpu_custom_call" | custom-call | flops 20000000000 | bytes 400000000 | tf_op jit(solution)/shard_map/pallas_call | solution.py:447
  155.1 0.0 copy-start
  155.1 1.6 copy-done
  156.7 0.0 copy-start.1
  156.7 1.6 copy-done.1
  158.3 0.0 copy-start.2
  158.3 1.2 copy-done.2
  159.5 13.7 %shard_map.78 = (f32[2048,512]{1,0:T(8,128)}, f32[1024,1024]{1,0:T(8,128)}) custom-call(f32[512,512]{1,0:T(8,128)S(1)} %copy-done.2, f32[2048,512]{1,0:T(8,128)} %get-tuple-element.9.yl, f32[2048,512]{1,0:T(8,128)} %get-tuple-element.10.u, f32[1024,512]{1,0:T(8,128)S(1)} %copy-done, f32[1024,1024]{1,0:T(8,128)} %get-tuple-element.12.v, f32[1024,512]{1,0:T(8,128)S(1)} %copy-done.1), custom_call_target="tpu_custom_call" | custom-call | tf_op jit(solution)/shard_map/pallas_call | solution.py:479
Async XLA Ops:
  155.1 1.6 copy-start
  156.7 1.6 copy-start.1
  158.3 1.2 copy-start.2

commit v3 on v2

--- a/solution.py
+++ b/solution.py
@@ -184,11 +184,6 @@
     for dx in (1, 3, 2):
         send(slot, slot, yls.at[3 + dx], ylr.at[((4 - dx) % 4) * 4 + 2], (a, vpos(dx, 0, 0)))
     send(slot, slot, yls.at[8], ylr.at[3], (a, vpos(0, 0, 1)))
-    slot = yr_slot(0, 1)
-    arrive(slot, yrr.at[1])
-    for dy in (1, 3, 2):
-        send(slot, slot, yrs.at[3 + dy], yrr.at[((4 - dy) % 4) * 2 + 1], (apos(dy, 0), t))
-
     across(0)
     in_plane(0)
     for dz in (0, 1):
@@ -274,6 +269,14 @@
     gram(ylt_h, ylt_l, gl)
     gram_left()
 
+    slot = yr_slot(0, 1)
+    arrive(slot, yrr.at[1])
+    for dy in (1, 3, 2):
+        send(slot, slot, yrs.at[3 + dy], yrr.at[((4 - dy) % 4) * 2 + 1], (apos(dy, 0), t))
+
+    across(1)
+    in_plane(1)
+
     for dz in (0, 1):
         for dy in (1, 3, 2):
             arrive(yr_slot(dy, dz), yrr.at[dy * 2 + dz])
@@ -283,8 +286,6 @@
     send(gr, gr_core, grs.at[0], grr.at[0], (a, vpos(0, 0, 1)))
 
     gram_right()
-    across(1)
-    in_plane(1)
     for copy in local_t + [local_u, local_v]:
         copy.wait()
     def right_sums(part):
@@ -388,22 +389,22 @@
     right_core(0)
     gram_pair_right()
     gram_pair_left()
-    left_pair(0)
-    right_pair(0)
+    right_sums(1)
     gram_spread_right()
     gram_spread_left()
-    right_sums(1)
     left_sums(1)
     right_core(1)
     merge_right()
+    left_pair(0)
+    right_pair(0)
     merge_left()
+    left_pair(1)
+    right_pair(1)
     left_spread(0)
     right_spread(0)
-    left_pair(1)
-    right_pair(1)
-    right_onward(0)
     left_spread(1)
     right_spread(1)
+    right_onward(0)
     right_onward(1)
     for part in range(2):
         left_done(part)
@@ -488,7 +489,7 @@
         ],
         out_specs=[pl.BlockSpec((512, 512), first), pl.BlockSpec((256, 1024), second)],
         scratch_shapes=[half(512, 512), half(512, 512), half(1024, 512), half(1024, 512)],
-        compiler_params=pltpu.CompilerParams(vmem_limit_bytes=48 * 2**20),
+        compiler_params=pltpu.CompilerParams(vmem_limit_bytes=60 * 2**20),
     )(w_left, yl_all, u_all, yr_all, v_all, w_right)
 
 

time: 174 us -> 168 us (0.966)
  local copies, waits for them, and re-layouts: 4.4 us -> 0 us
    unnamed x6 -> x0, local copies, waits for them, and re-layouts: 4.4 us -> none
    pallas_call x1, Pallas kernels: 154 us -> 151 us  [shards(): pl.pallas_call(move_kernel, out_shape=[shape((2048, 512), f32), shape((10...]
    pallas_call x1, Pallas kernels: 13.7 us -> 15.7 us  [shards(): pl.pallas_call(update_kernel, grid=(8,), out_shape=[shape((2048, 512), f3...]
where the time goes in v3:
time: 168 us; the launch traced here: 167 us
  Pallas kernels  167 us (99%)
    pallas_call x1, Pallas kernels, shards(): pl.pallas_call(move_kernel, out_shape=[shape((2048, 512), f32), shape((10...  151 us
    pallas_call x1, Pallas kernels, shards(): pl.pallas_call(update_kernel, grid=(8,), out_shape=[shape((2048, 512), f3...  15.7 us

profile of v3, /device:TPU:1, one launch (start us, length us, event | category | flops | bytes accessed | tf_op | source)
XLA Modules:
  0.0 167.5 jit_solution(6104061844328136383)
XLA Ops:
  0.6 151.2 %shard_map.77 = (f32[2048,512]{1,0:T(8,128)}, f32[1024,1024]{1,0:T(8,128)}, f32[2048,512]{1,0:T(8,128)}, f32[1024,512]{1,0:T(8,128)}, f32[512,512]{1,0:T(8,128)}, /*index=5*/f32[1024,512]{1,0:T(8,128)}) custom-call(f32[4,128,128]{2,1,0:T(8,128)} %yl.1, f32[4,128,128]{2,1,0:T(8,128)} %yr.1, f32[128,8192]{1,0:T(8,128)} %u.1, f32[128,8192]{1,0:T(8,128)} %v.1, ...), custom_call_target="tpu_custom_call" | custom-call | flops 20000000000 | bytes 400000000 | tf_op jit(solution)/shard_map/pallas_call | solution.py:448
  151.8 15.7 %shard_map.78 = (f32[2048,512]{1,0:T(8,128)}, f32[1024,1024]{1,0:T(8,128)}) custom-call(f32[512,512]{1,0:T(8,128)} %get-tuple-element.8.wl, f32[2048,512]{1,0:T(8,128)} %get-tuple-element.9.yl, f32[2048,512]{1,0:T(8,128)} %get-tuple-element.10.u, f32[1024,512]{1,0:T(8,128)} %get-tuple-element.11.yr, f32[1024,1024]{1,0:T(8,128)} %get-tuple-element.12.v, ...), custom_call_target="tpu_custom_call" | custom-call | tf_op jit(solution)/shard_map/pallas_call | solution.py:480

commit v4 on v3

--- a/solution.py
+++ b/solution.py
@@ -34,7 +34,7 @@
 
 
 def exact(a, b):
-    return jnp.dot(a, b, precision=lax.Precision.HIGHEST, preferred_element_type=f32)
+    return three(*split(a), *split(b))
 
 
 def aligned(index, size):
@@ -56,8 +56,9 @@
     for p in (3, 2, 1, 0):
         unit = (lax.broadcasted_iota(jnp.int32, (128, 512), 0) + p * 128
                 == lax.broadcasted_iota(jnp.int32, (128, 512), 1)).astype(f32)
-        for q in range(p + 1, 4):
-            unit = unit - exact(grams[PAIRS.index((p, q))], rows[q])
+        if p < 3:
+            beside = jnp.concatenate([grams[PAIRS.index((p, q))] for q in range(p + 1, 4)], axis=1)
+            unit = unit - exact(beside, jnp.concatenate(rows[p + 1:], axis=0))
         rows[p] = exact(factors[p], unit)
     return jnp.concatenate(rows, axis=0)
 
@@ -395,15 +396,15 @@
     left_sums(1)
     right_core(1)
     merge_right()
+    right_pair(0)
     left_pair(0)
-    right_pair(0)
     merge_left()
+    right_pair(1)
     left_pair(1)
-    right_pair(1)
+    right_spread(0)
     left_spread(0)
-    right_spread(0)
+    right_spread(1)
     left_spread(1)
-    right_spread(1)
     right_onward(0)
     right_onward(1)
     for part in range(2):

time: 168 us -> 165 us (0.982)
  Pallas kernels: 167 us -> 164 us
    pallas_call x1, Pallas kernels: 151 us -> 149 us  [shards(): pl.pallas_call(move_kernel, out_shape=[shape((2048, 512), f32), shape((10...]
where the time goes in v4:
time: 165 us
  Pallas kernels  164 us (99%)
    pallas_call x1, Pallas kernels, shards(): pl.pallas_call(move_kernel, out_shape=[shape((2048, 512), f32), shape((10...  149 us
    pallas_call x1, Pallas kernels, shards(): pl.pallas_call(update_kernel, grid=(8,), out_shape=[shape((2048, 512), f3...  15.7 us

profile of v4, /device:TPU:1, one launch (start us, length us, event | category | flops | bytes accessed | tf_op | source)
XLA Modules:
  0.0 164.9 jit_solution(2378611420899614631)
XLA Ops:
  0.6 148.6 %shard_map.77 = (f32[2048,512]{1,0:T(8,128)}, f32[1024,1024]{1,0:T(8,128)}, f32[2048,512]{1,0:T(8,128)}, f32[1024,512]{1,0:T(8,128)}, f32[512,512]{1,0:T(8,128)}, /*index=5*/f32[1024,512]{1,0:T(8,128)}) custom-call(f32[4,128,128]{2,1,0:T(8,128)} %yl.1, f32[4,128,128]{2,1,0:T(8,128)} %yr.1, f32[128,8192]{1,0:T(8,128)} %u.1, f32[128,8192]{1,0:T(8,128)} %v.1, ...), custom_call_target="tpu_custom_call" | custom-call | flops 20000000000 | bytes 400000000 | tf_op jit(solution)/shard_map/pallas_call | solution.py:449
  149.2 15.7 %shard_map.78 = (f32[2048,512]{1,0:T(8,128)}, f32[1024,1024]{1,0:T(8,128)}) custom-call(f32[512,512]{1,0:T(8,128)} %get-tuple-element.8.wl, f32[2048,512]{1,0:T(8,128)} %get-tuple-element.9.yl, f32[2048,512]{1,0:T(8,128)} %get-tuple-element.10.u, f32[1024,512]{1,0:T(8,128)} %get-tuple-element.11.yr, f32[1024,1024]{1,0:T(8,128)} %get-tuple-element.12.v, ...), custom_call_target="tpu_custom_call" | custom-call | tf_op jit(solution)/shard_map/pallas_call | solution.py:481

commit v5 on v4

--- a/solution.py
+++ b/solution.py
@@ -480,15 +480,15 @@
     whole = lambda i: (0, 0)
     return pl.pallas_call(
         update_kernel,
-        grid=(8,),
+        grid=(6,),
         out_shape=[shape((2048, 512), f32), shape((1024, 1024), f32)],
         in_specs=[
             pl.BlockSpec((512, 512), whole),
             pl.BlockSpec((512, 512), first), pl.BlockSpec((512, 512), first),
-            pl.BlockSpec((256, 512), second), pl.BlockSpec((256, 1024), second),
+            pl.BlockSpec((512, 512), second), pl.BlockSpec((512, 1024), second),
             pl.BlockSpec((1024, 512), whole),
         ],
-        out_specs=[pl.BlockSpec((512, 512), first), pl.BlockSpec((256, 1024), second)],
+        out_specs=[pl.BlockSpec((512, 512), first), pl.BlockSpec((512, 1024), second)],
         scratch_shapes=[half(512, 512), half(512, 512), half(1024, 512), half(1024, 512)],
         compiler_params=pltpu.CompilerParams(vmem_limit_bytes=60 * 2**20),
     )(w_left, yl_all, u_all, yr_all, v_all, w_right)

time: 165 us -> 165 us (level)
  no operation moved by 1% of the time
where the time goes in v5:
time: 165 us; the launch traced here: 164 us
  Pallas kernels  164 us (99%)
    pallas_call x1, Pallas kernels, shards(): pl.pallas_call(move_kernel, out_shape=[shape((2048, 512), f32), shape((10...  149 us
    pallas_call x1, Pallas kernels, shards(): pl.pallas_call(update_kernel, grid=(6,), out_shape=[shape((2048, 512), f3...  15.2 us

profile of v5, /device:TPU:1, one launch (start us, length us, event | category | flops | bytes accessed | tf_op | source)
XLA Modules:
  0.0 164.4 jit_solution(3517333793783908860)
XLA Ops:
  0.6 148.6 %shard_map.77 = (f32[2048,512]{1,0:T(8,128)}, f32[1024,1024]{1,0:T(8,128)}, f32[2048,512]{1,0:T(8,128)}, f32[1024,512]{1,0:T(8,128)}, f32[512,512]{1,0:T(8,128)}, /*index=5*/f32[1024,512]{1,0:T(8,128)}) custom-call(f32[4,128,128]{2,1,0:T(8,128)} %yl.1, f32[4,128,128]{2,1,0:T(8,128)} %yr.1, f32[128,8192]{1,0:T(8,128)} %u.1, f32[128,8192]{1,0:T(8,128)} %v.1, ...), custom_call_target="tpu_custom_call" | custom-call | flops 20000000000 | bytes 400000000 | tf_op jit(solution)/shard_map/pallas_call | solution.py:449
  149.2 15.2 %shard_map.78 = (f32[2048,512]{1,0:T(8,128)}, f32[1024,1024]{1,0:T(8,128)}) custom-call(f32[512,512]{1,0:T(8,128)} %get-tuple-element.8.wl, f32[2048,512]{1,0:T(8,128)} %get-tuple-element.9.yl, f32[2048,512]{1,0:T(8,128)} %get-tuple-element.10.u, f32[1024,512]{1,0:T(8,128)} %get-tuple-element.11.yr, f32[1024,1024]{1,0:T(8,128)} %get-tuple-element.12.v, ...), custom_call_target="tpu_custom_call" | custom-call | tf_op jit(solution)/shard_map/pallas_call | solution.py:481

commit v6 on v5

--- a/solution.py
+++ b/solution.py
@@ -51,16 +51,17 @@
     return ((4 - dx) % 4, dz, dc)
 
 
-def merged(factors, grams):
-    rows = [None] * 4
+def merged(*sides):
+    rows = [[None] * 4 for _ in sides]
     for p in (3, 2, 1, 0):
-        unit = (lax.broadcasted_iota(jnp.int32, (128, 512), 0) + p * 128
-                == lax.broadcasted_iota(jnp.int32, (128, 512), 1)).astype(f32)
-        if p < 3:
-            beside = jnp.concatenate([grams[PAIRS.index((p, q))] for q in range(p + 1, 4)], axis=1)
-            unit = unit - exact(beside, jnp.concatenate(rows[p + 1:], axis=0))
-        rows[p] = exact(factors[p], unit)
-    return jnp.concatenate(rows, axis=0)
+        for done, (factors, grams) in zip(rows, sides):
+            unit = (lax.broadcasted_iota(jnp.int32, (128, 512), 0) + p * 128
+                    == lax.broadcasted_iota(jnp.int32, (128, 512), 1)).astype(f32)
+            if p < 3:
+                beside = jnp.concatenate([grams[PAIRS.index((p, q))] for q in range(p + 1, 4)], axis=1)
+                unit = unit - exact(beside, jnp.concatenate(done[p + 1:], axis=0))
+            done[p] = exact(factors[p], unit)
+    return [jnp.concatenate(done, axis=0) for done in rows]
 
 
 def upper(t):
@@ -251,17 +252,16 @@
         for dx in (1, 3, 2):
             send(spot_r, spot_r, grs.at[4 + dx], grr.at[4 + (4 - dx) % 4], (a, vpos(dx, 0, 0)))
 
-    def merge_left():
-        for dy in (1, 2, 3):
-            arrive(gl_all.at[aligned(lax.rem(y + dy, 4), 192), :], glr.at[4 + dy])
-        tl_h[...], tl_l[...] = split(merged(
-            [upper(tl[p]) for p in range(4)], [gl_all[pl.ds(i * 128, 128), :] for i in range(6)]))
-
-    def merge_right():
-        for dx in (1, 2, 3):
-            arrive(gr_all.at[aligned(lax.rem(x + dx, 4), 192), :], grr.at[4 + dx])
-        tr_h[...], tr_l[...] = split(merged(
-            [upper(tr[p]).T for p in range(4)], [gr_all[pl.ds(i * 128, 128), :] for i in range(6)]))
+    def merge_both():
+        for d in (1, 2, 3):
+            arrive(gr_all.at[aligned(lax.rem(x + d, 4), 192), :], grr.at[4 + d])
+            arrive(gl_all.at[aligned(lax.rem(y + d, 4), 192), :], glr.at[4 + d])
+        right, left = merged(
+            ([upper(tr[p]).T for p in range(4)], [gr_all[pl.ds(i * 128, 128), :] for i in range(6)]),
+            ([upper(tl[p]) for p in range(4)], [gl_all[pl.ds(i * 128, 128), :] for i in range(6)]),
+        )
+        tr_h[...], tr_l[...] = split(right)
+        tl_h[...], tl_l[...] = split(left)
 
     for o in range(1, 16, 2):
         arrive(yl_slot(o // 4, (o // 2) % 2, 1), ylr.at[o])
@@ -395,10 +395,9 @@
     gram_spread_left()
     left_sums(1)
     right_core(1)
-    merge_right()
     right_pair(0)
     left_pair(0)
-    merge_left()
+    merge_both()
     right_pair(1)
     left_pair(1)
     right_spread(0)
@@ -418,15 +417,18 @@
         copy.wait()
 
 
-def update_kernel(wl, yl, u, yr, v, wr, u_out, v_out, wl_h, wl_l, wr_h, wr_l):
+def update_kernel(wl, yl, u, yr, v, wr_in, u_out, v_out, wl_h, wl_l, wr_h, wr_l, wr, sem):
     step = pl.program_id(0)
+    copy = pltpu.make_async_copy(wr_in, wr, sem)
 
     @pl.when(step == 0)
     def _():
+        copy.start()
         wl_h[...], wl_l[...] = split(wl[...])
 
     @pl.when(step == 4)
     def _():
+        copy.wait()
         wr_h[...], wr_l[...] = split(wr[...])
 
     @pl.when(step < 4)
@@ -486,10 +488,10 @@
             pl.BlockSpec((512, 512), whole),
             pl.BlockSpec((512, 512), first), pl.BlockSpec((512, 512), first),
             pl.BlockSpec((512, 512), second), pl.BlockSpec((512, 1024), second),
-            pl.BlockSpec((1024, 512), whole),
+            any_space,
         ],
         out_specs=[pl.BlockSpec((512, 512), first), pl.BlockSpec((512, 1024), second)],
-        scratch_shapes=[half(512, 512), half(512, 512), half(1024, 512), half(1024, 512)],
+        scratch_shapes=[half(512, 512), half(512, 512), half(1024, 512), half(1024, 512), buf(1024, 512), dma],
         compiler_params=pltpu.CompilerParams(vmem_limit_bytes=60 * 2**20),
     )(w_left, yl_all, u_all, yr_all, v_all, w_right)
 

time: 165 us -> 163 us (0.988)
  Pallas kernels: 164 us -> 162 us
where the time goes in v6:
time: 163 us
  Pallas kernels  162 us (99%)
    pallas_call x1, Pallas kernels, shards(): pl.pallas_call(move_kernel, out_shape=[shape((2048, 512), f32), shape((10...  148 us
    pallas_call x1, Pallas kernels, shards(): pl.pallas_call(update_kernel, grid=(6,), out_shape=[shape((2048, 512), f3...  14.6 us

profile of v6, /device:TPU:1, one launch (start us, length us, event | category | flops | bytes accessed | tf_op | source)
XLA Modules:
  0.0 163.2 jit_solution(10713430456993999814)
XLA Ops:
  0.6 147.8 %shard_map.77 = (f32[2048,512]{1,0:T(8,128)}, f32[1024,1024]{1,0:T(8,128)}, f32[2048,512]{1,0:T(8,128)}, f32[1024,512]{1,0:T(8,128)}, f32[512,512]{1,0:T(8,128)}, /*index=5*/f32[1024,512]{1,0:T(8,128)}) custom-call(f32[4,128,128]{2,1,0:T(8,128)} %yl.1, f32[4,128,128]{2,1,0:T(8,128)} %yr.1, f32[128,8192]{1,0:T(8,128)} %u.1, f32[128,8192]{1,0:T(8,128)} %v.1, ...), custom_call_target="tpu_custom_call" | custom-call | flops 20000000000 | bytes 400000000 | tf_op jit(solution)/shard_map/pallas_call | solution.py:451
  148.5 14.6 %shard_map.78 = (f32[2048,512]{1,0:T(8,128)}, f32[1024,1024]{1,0:T(8,128)}) custom-call(f32[512,512]{1,0:T(8,128)} %get-tuple-element.8.wl, f32[2048,512]{1,0:T(8,128)} %get-tuple-element.9.yl, f32[2048,512]{1,0:T(8,128)} %get-tuple-element.10.u, f32[1024,512]{1,0:T(8,128)} %get-tuple-element.11.yr, f32[1024,1024]{1,0:T(8,128)} %get-tuple-element.12.v, ...), custom_call_target="tpu_custom_call" | custom-call | tf_op jit(solution)/shard_map/pallas_call | solution.py:483

commit v7 on v6

--- a/solution.py
+++ b/solution.py
@@ -392,8 +392,8 @@
     gram_pair_left()
     right_sums(1)
     gram_spread_right()
+    left_sums(1)
     gram_spread_left()
-    left_sums(1)
     right_core(1)
     right_pair(0)
     left_pair(0)

time: 163 us -> 167 us (1.025); the launches traced: 163 us -> 165 us
  Pallas kernels: 162 us -> 164 us
    pallas_call x1, Pallas kernels: 148 us -> 150 us  [shards(): pl.pallas_call(move_kernel, out_shape=[shape((2048, 512), f32), shape((10...]
where the time goes in v7:
time: 167 us; the launch traced here: 165 us
  Pallas kernels  164 us (98%)
    pallas_call x1, Pallas kernels, shards(): pl.pallas_call(move_kernel, out_shape=[shape((2048, 512), f32), shape((10...  150 us
    pallas_call x1, Pallas kernels, shards(): pl.pallas_call(update_kernel, grid=(6,), out_shape=[shape((2048, 512), f3...  14.6 us

profile of v7, /device:TPU:1, one launch (start us, length us, event | category | flops | bytes accessed | tf_op | source)
XLA Modules:
  0.0 165.1 jit_solution(17767269262254201044)
XLA Ops:
  0.6 149.8 %shard_map.77 = (f32[2048,512]{1,0:T(8,128)}, f32[1024,1024]{1,0:T(8,128)}, f32[2048,512]{1,0:T(8,128)}, f32[1024,512]{1,0:T(8,128)}, f32[512,512]{1,0:T(8,128)}, /*index=5*/f32[1024,512]{1,0:T(8,128)}) custom-call(f32[4,128,128]{2,1,0:T(8,128)} %yl.1, f32[4,128,128]{2,1,0:T(8,128)} %yr.1, f32[128,8192]{1,0:T(8,128)} %u.1, f32[128,8192]{1,0:T(8,128)} %v.1, ...), custom_call_target="tpu_custom_call" | custom-call | flops 20000000000 | bytes 400000000 | tf_op jit(solution)/shard_map/pallas_call | solution.py:451
  150.4 14.6 %shard_map.78 = (f32[2048,512]{1,0:T(8,128)}, f32[1024,1024]{1,0:T(8,128)}) custom-call(f32[512,512]{1,0:T(8,128)} %get-tuple-element.8.wl, f32[2048,512]{1,0:T(8,128)} %get-tuple-element.9.yl, f32[2048,512]{1,0:T(8,128)} %get-tuple-element.10.u, f32[1024,512]{1,0:T(8,128)} %get-tuple-element.11.yr, f32[1024,1024]{1,0:T(8,128)} %get-tuple-element.12.v, ...), custom_call_target="tpu_custom_call" | custom-call | tf_op jit(solution)/shard_map/pallas_call | solution.py:483
